TPU v7x, 128 devices: a whole 4x4x4 slice. The times are simulated.
128 devices in a mesh: box: 32 (over y, z, core), sx: 2 (over x_lo), sy: 2 (over x_hi).
Axes of the slice: x: 4 (x_hi: 2, x_lo: 2; x = x_hi * 2 + x_lo), y: 4, z: 4, core: 2. Of those that a mesh axis runs over, the one named last changes fastest.
Arguments:
- coarse: float32 [256, 96, 128], P('box'), may hold values from -4 to 4
- anchors: int32 [32, 3], replicated, may hold values from 0 to 234, as said below
- dielectric: float32 [32, 80, 64, 256], P('box', 'sx', 'sy'), may hold values from 0.5 to 4
- screening: float32 [32, 80, 64, 256], P('box', 'sx', 'sy'), may hold values from 0.2 to 2
- source: float32 [32, 80, 64, 256], P('box', 'sx', 'sy'), may hold values from -40 to 40
Outputs:
- potential: float32 [32, 80, 64, 256], P('box', 'sx', 'sy')
- box_norm: float32 [32], P('box')
Inputs may be any that keep to these rules, and one draw needn't show every extreme that they name: `anchors`: column 0 of each row is at most 234, column 1 at most 78, column 2 at most 62; some box reaches all three of these, and some box begins at coarse cell 0 in every dimension.
All inputs are finite; a program needn't handle non-finite values.
Results may differ from a plain program's by a relative error of at most 0.000098.
Values sent between devices are 32-bit elements; how exact they have to be, the bound alone decides.
A program may use at most 128 MiB of HBM per device.

v0:
```python
import jax
import jax.numpy as jnp
from jax import lax
from jax.sharding import PartitionSpec as P

RATIO = 4
SWEEPS = 2


def padded_2(block, sides, width):
    for axis, dim in sides:
        count = lax.axis_size(axis)
        forward = [(i, i + 1) for i in range(count - 1)]
        backward = [(target, source) for source, target in forward]
        low = lax.ppermute(
            lax.slice_in_dim(block, block.shape[dim] - width, None, axis=dim), axis, forward
        )
        high = lax.ppermute(lax.slice_in_dim(block, 0, width, axis=dim), axis, backward)
        block = jnp.concatenate([low, block, high], axis=dim)
    return block


def spread(leading, amount, extent):
    fine_index = leading + jnp.arange(amount, dtype=jnp.int32)
    shifted = fine_index + 1
    lower = jnp.clip(shifted // RATIO, 0, extent - 2)
    fraction = jnp.clip((shifted - lower * RATIO).astype(jnp.float32) / RATIO, 0.0, 1.0)
    columns = jnp.arange(extent, dtype=jnp.int32)[None, :]
    below = jnp.where(columns == lower[:, None], 1.0 - fraction[:, None], 0.0)
    above = jnp.where(columns == lower[:, None] + 1, fraction[:, None], 0.0)
    return below + above


def interpolate(coarse_block, rows_x, rows_y, rows_z):
    precise = lax.Precision.HIGHEST
    sectioned = jnp.einsum("abc,kc->abk", coarse_block, rows_z, precision=precise)
    sectioned = jnp.einsum("abk,jb->ajk", sectioned, rows_y, precision=precise)
    return jnp.einsum("ajk,ia->ijk", sectioned, rows_x, precision=precise)


def neighbours(values):
    return [
        values[2:, 1:-1, 1:-1],
        values[:-2, 1:-1, 1:-1],
        values[1:-1, 2:, 1:-1],
        values[1:-1, :-2, 1:-1],
        values[1:-1, 1:-1, 2:],
        values[1:-1, 1:-1, :-2],
    ]


def balance(values, dielectric_pad, screening, charge):
    centre = values[1:-1, 1:-1, 1:-1]
    own_dielectric = dielectric_pad[1:-1, 1:-1, 1:-1]
    flux_sum = jnp.zeros_like(centre)
    weights = jnp.zeros_like(centre)
    for near_value, near_dielectric in zip(neighbours(values), neighbours(dielectric_pad)):
        coupling = 0.5 * (own_dielectric + near_dielectric)
        flux_sum = flux_sum + coupling * (centre - near_value)
        weights = weights + coupling
    residual = flux_sum + screening * jnp.sinh(centre) - charge
    return (residual, weights, centre)


def smooth(values, dielectric_pad, screening, charge, active):
    residual, weights, centre = balance(values, dielectric_pad, screening, charge)
    updated = jnp.where(
        active, centre - residual / (weights + screening * jnp.cosh(centre)), centre
    )
    return values.at[1:-1, 1:-1, 1:-1].set(updated)


def body(coarse, anchors, dielectric, screening, source):
    precise = lax.Precision.HIGHEST
    tile_x = dielectric.shape[1]
    tile_y = dielectric.shape[2]
    depth_z = dielectric.shape[3]
    box_x = tile_x * lax.axis_size("sx")
    box_y = tile_y * lax.axis_size("sy")
    extent_x = (box_x + 1) // RATIO + 2
    extent_y = (box_y + 1) // RATIO + 2
    extent_z = (depth_z + 1) // RATIO + 2
    box_index = lax.axis_index("box")
    anchor = lax.dynamic_slice_in_dim(anchors, box_index, 1, 0)[0]
    corner_x = anchor[0]
    corner_y = anchor[1]
    corner_z = anchor[2]
    portion = lax.all_gather(coarse, "box", axis=0, tiled=True)
    row_count = portion.shape[0]
    window = lax.dynamic_slice(portion, (0, corner_y, corner_z), (row_count, extent_y, extent_z))
    select = (
        corner_x + jnp.arange(extent_x, dtype=jnp.int32)[:, None]
        == jnp.arange(row_count, dtype=jnp.int32)[None, :]
    ).astype(jnp.float32)
    coarse_block = jnp.einsum("ar,rbc->abc", select, window, precision=precise)
    margin = 1
    start_x = lax.axis_index("sx") * tile_x
    start_y = lax.axis_index("sy") * tile_y
    initial = interpolate(
        coarse_block,
        spread(start_x - margin, tile_x + 2 * margin, extent_x),
        spread(start_y - margin, tile_y + 2 * margin, extent_y),
        spread(-1, depth_z + 2, extent_z),
    )
    potential = initial[margin:-margin, margin:-margin]
    global_x = start_x - margin + jnp.arange(tile_x + 2 * margin, dtype=jnp.int32)
    global_y = start_y - margin + jnp.arange(tile_y + 2 * margin, dtype=jnp.int32)
    inside = ((global_x >= 0) & (global_x < box_x))[:, None, None] & (
        (global_y >= 0) & (global_y < box_y)
    )[None, :, None]
    parity = (
        global_x[:, None, None]
        + global_y[None, :, None]
        + jnp.arange(depth_z, dtype=jnp.int32)[None, None, :]
    ) % 2
    dielectric_pad = jnp.pad(dielectric[0], ((0, 0), (0, 0), (1, 1)))
    screening_tile = screening[0]
    charge_tile = source[0]
    dielectric_ext = padded_2(dielectric_pad, (("sx", 0), ("sy", 1)), 1)

    def extend(values):
        padded = padded_2(values, (("sx", 0), ("sy", 1)), 1)
        return jnp.where(inside, padded, initial)

    for repeat in range(SWEEPS):
        for colour in (0, 1):
            padded = smooth(
                extend(potential),
                dielectric_ext,
                screening_tile,
                charge_tile,
                parity[1:-1, 1:-1] == colour,
            )
            potential = padded[1:-1, 1:-1]
    residual = balance(extend(potential), dielectric_ext, screening_tile, charge_tile)[0]
    own_squares = jnp.sum(residual * residual)
    group_total = lax.psum(own_squares, ("sx", "sy"))
    box_norm = jnp.sqrt(group_total / (box_x * box_y * depth_z) + 1e-06)
    return (potential[:, :, 1:-1][None], box_norm.reshape(1))


def solution(mesh):
    in_specs = (
        P("box", None, None),
        P(),
        P("box", "sx", "sy", None),
        P("box", "sx", "sy", None),
        P("box", "sx", "sy", None),
    )
    out_specs = (P("box", "sx", "sy", None), P("box"))
    return jax.shard_map(body, mesh=mesh, in_specs=in_specs, out_specs=out_specs, check_vma=False)
```

profile of v0, /device:TPU:96, one launch (start us, length us, event | category | flops | bytes accessed | tf_op | source)
XLA Modules:
  0.0 323.8 jit_solution(13236844155144270666)
XLA Ops:
  7.9 2.1 copy.49
  10.0 1.0 pad_slice_fusion
  11.1 3.4 %collective-permute-start.5 = (f32[1,32,258]{2,0,1:T(1,128)}, f32[1,32,258]{2,0,1:T(1,128)S(1)}, u32[]{:S(2)}, u32[]{:S(2)}) collective-permute-start(f32[1,32,258]{2,0,1:T(1,128)} %get-tuple-element.86), channel_id=1, source_target_pairs={{0,2},{1,3},{4,6},{5,7},{8,10},{9,11},{12,14},{13,15},{16,18},{17,... | collective-permute-start | bytes 99080 | tf_op jit(solution)/shard_map/ppermute | solution.py:15
  14.5 1.3 collective-permute-start.4
  21.6 1.4 negate_select_fusion
  23.1 51.0 %all-gather.2.cloned.1.call-done = f32[256,96,128]{2,1,0:T(8,128)} async-done(((f32[8,96,128]{2,1,0:T(8,128)}), f32[256,96,128]{2,1,0:T(8,128)}) %all-gather.2.cloned.1.call-update) | async-done | bytes 12582928 | tf_op jit(solution)/shard_map/all_gather | solution.py:88
  74.1 3.1 constant_dynamic-slice_fusion
  77.2 1.1 fusion
  79.2 1.3 fusion.117
  80.5 2.2 fusion.101
  82.7 3.4 %collective-permute-start = (f32[1,32,258]{2,0,1:T(1,128)S(1)}, f32[1,32,258]{2,0,1:T(1,128)S(1)}, u32[]{:S(2)}, u32[]{:S(2)}) collective-permute-start(f32[1,32,258]{2,0,1:T(1,128)S(1)} %get-tuple-element.72), channel_id=1, source_target_pairs={{0,2},{1,3},{4,6},{5,7},{8,10},{9,11},{12,14},{13,15},{16,18},{17,... | collective-permute-start | bytes 99080 | tf_op jit(solution)/shard_map/ppermute | solution.py:15
  86.1 1.3 collective-permute-start.1
  88.2 3.9 %collective-permute-done.1 = f32[1,32,258]{2,0,1:T(1,128)S(1)} collective-permute-done((f32[1,32,258]{2,0,1:T(1,128)S(1)}, f32[1,32,258]{2,0,1:T(1,128)S(1)}, u32[]{:S(2)}, u32[]{:S(2)}) %collective-permute-start.1) | collective-permute-done | bytes 33056 | tf_op jit(solution)/shard_map/ppermute | solution.py:18
  92.1 4.6 %collective-permute-start.2 = (f32[42,1,258]{2,0,1:T(8,128)S(1)}, f32[42,1,258]{2,0,1:T(8,128)S(1)}, u32[]{:S(2)}, u32[]{:S(2)}) collective-permute-start(f32[42,1,258]{2,0,1:T(8,128)S(1)} %get-tuple-element.84), channel_id=1, source_target_pairs={{0,1},{2,3},{4,5},{6,7},{8,9},{10,11},{12,13},{14,15},{16,17},{18,... | collective-permute-start | bytes 130040 | tf_op jit(solution)/shard_map/ppermute | solution.py:15
  96.7 1.3 collective-permute-start.3
  98.1 6.7 %collective-permute-start.7 = (f32[42,1,258]{2,0,1:T(8,128)S(1)}, f32[42,1,258]{2,0,1:T(8,128)}, u32[]{:S(2)}, u32[]{:S(2)}) collective-permute-start(f32[42,1,258]{2,0,1:T(8,128)S(1)} %get-tuple-element.82), channel_id=1, source_target_pairs={{0,1},{2,3},{4,5},{6,7},{8,9},{10,11},{12,13},{14,15},{16,17},{18,... | collective-permute-start | bytes 130040 | tf_op jit(solution)/shard_map/ppermute | solution.py:15
  104.8 1.7 collective-permute-start.6
  106.5 1.1 maximum_select_fusion
  107.6 5.3 %collective-permute-done.6 = f32[42,1,258]{2,0,1:T(8,128)} collective-permute-done((f32[42,1,258]{2,0,1:T(8,128)S(1)}, f32[42,1,258]{2,0,1:T(8,128)}, u32[]{:S(2)}, u32[]{:S(2)}) %collective-permute-start.6) | collective-permute-done | bytes 43376 | tf_op jit(solution)/shard_map/ppermute | solution.py:18
  112.9 13.0 %subtract_select_fusion.3 = (f32[40,32,256]{2,0,1:T(8,128)}, f32[40,32,256]{2,0,1:T(8,128)}, f32[40,32,256]{2,0,1:T(8,128)}, f32[40,32,256]{2,0,1:T(8,128)}, f32...) fusion(f32[42,34,258]{2,0,1:T(8,128)S(1)} %maximum_select_fusion, ...), kind=kLoop, calls=%fused_computation.15 | loop fusion | flops 22937600 | bytes 27032736 | tf_op jit(solution)/shard_map/jit(_where)/select_n | solution.py:67
  125.9 18.2 %scatter.14 = f32[42,34,258]{2,0,1:T(8,128)} dynamic-update-slice(f32[42,34,258]{2,0,1:T(8,128)} %copy-done.2, f32[40,32,256]{2,0,1:T(8,128)} %get-tuple-element.56, s32[]{:T(128)} %constant.184.clone.1, s32[]{:T(128)} %constant.184.clone.1, s32[]{:T(128)} %constant.184.clone.1) | dynamic-update-slice | bytes 2621444 | tf_op jit(solution)/shard_map/scatter | solution.py:70
  144.1 1.2 fusion.153
  145.3 1.3 collective-permute-start.8
  146.6 1.3 collective-permute-start.9
  147.9 2.0 slice.472
  149.9 2.9 collective-permute-done.9
  152.8 2.3 collective-permute-start.10
  155.1 1.6 collective-permute-start.11
  157.1 6.1 %collective-permute-done.11 = f32[42,1,258]{2,0,1:T(8,128)S(1)} collective-permute-done((f32[42,1,258]{2,0,1:T(8,128)S(1)}, f32[42,1,258]{2,0,1:T(8,128)S(1)}, u32[]{:S(2)}, u32[]{:S(2)}) %collective-permute-start.11) | collective-permute-done | bytes 43376 | tf_op jit(solution)/shard_map/ppermute | solution.py:18
  164.3 6.6 %subtract_select_fusion.2 = (f32[40,32,256]{2,0,1:T(8,128)}, pred[40,32,256]{2,0,1:T(8,128)(4,1)S(1)}) fusion(f32[40,32,256]{2,0,1:T(8,128)S(1)} %copy-done.36, f32[42,34,258]{2,0,1:T(8,128)S(1)} %maximum_select_fusion.1, f32[40,32,256]{2,0,1:T(8,128)S(1)} %copy-done.32, f32[40,32,256]{2,0,1:T(8,128)S(1)} %copy-done.28, f32[40,32,256]{2,0,1:T(8,128)S(1)} %copy-done.24, ...), kind=kLoop, calls=%fused_computation.13 | loop fusion | flops 16384000 | bytes 22937600 | tf_op jit(solution)/shard_map/jit(_where)/select_n | solution.py:67
  170.9 18.2 %scatter.15 = f32[42,34,258]{2,0,1:T(8,128)} dynamic-update-slice(f32[42,34,258]{2,0,1:T(8,128)} %copy-done.3, f32[40,32,256]{2,0,1:T(8,128)} %get-tuple-element.54, s32[]{:T(128)} %constant.184.clone.1, s32[]{:T(128)} %constant.184.clone.1, s32[]{:T(128)} %constant.184.clone.1) | dynamic-update-slice | bytes 2621444 | tf_op jit(solution)/shard_map/scatter | solution.py:70
  189.1 1.2 fusion.152
  190.3 1.3 collective-permute-start.12
  191.6 1.3 collective-permute-start.13
  192.9 1.9 slice.482
  194.8 2.7 collective-permute-done.13
  197.6 2.3 collective-permute-start.14
  199.9 1.8 collective-permute-start.15
  201.8 6.1 %collective-permute-done.15 = f32[42,1,258]{2,0,1:T(8,128)S(1)} collective-permute-done((f32[42,1,258]{2,0,1:T(8,128)S(1)}, f32[42,1,258]{2,0,1:T(8,128)S(1)}, u32[]{:S(2)}, u32[]{:S(2)}) %collective-permute-start.15) | collective-permute-done | bytes 43376 | tf_op jit(solution)/shard_map/ppermute | solution.py:18
  209.0 1.4 copy-done.5
  210.5 5.9 %subtract_select_fusion.1 = f32[40,32,256]{2,0,1:T(8,128)} fusion(pred[40,32,256]{2,0,1:T(8,128)(4,1)S(1)} %copy-done.44, f32[40,32,256]{2,0,1:T(8,128)S(1)} %copy-done.37, f32[42,34,258]{2,0,1:T(8,128)S(1)} %maximum_select_fusion.2, f32[40,32,256]{2,0,1:T(8,128)S(1)} %copy-done.33, f32[40,32,256]{2,0,1:T(8,128)S(1)} %copy-done.29, ...), kind=kLoop, calls=%fused_computation.11 | loop fusion | flops 13434880 | bytes 21299200 | tf_op jit(solution)/shard_map/jit(_where)/select_n | solution.py:67
  216.4 18.2 %scatter.16 = f32[42,34,258]{2,0,1:T(8,128)} dynamic-update-slice(f32[42,34,258]{2,0,1:T(8,128)} %copy-done.5, f32[40,32,256]{2,0,1:T(8,128)} %subtract_select_fusion.1, s32[]{:T(128)} %constant.184.clone.1, s32[]{:T(128)} %constant.184.clone.1, s32[]{:T(128)} %constant.184.clone.1) | dynamic-update-slice | bytes 2621444 | tf_op jit(solution)/shard_map/scatter | solution.py:70
  234.6 1.2 fusion.151
  235.8 1.3 collective-permute-start.16
  237.1 1.3 collective-permute-start.17
  238.4 1.9 slice.492
  240.3 2.7 collective-permute-done.17
  243.1 2.3 collective-permute-start.18
  245.4 1.6 collective-permute-start.19
  247.3 6.1 %collective-permute-done.19 = f32[42,1,258]{2,0,1:T(8,128)S(1)} collective-permute-done((f32[42,1,258]{2,0,1:T(8,128)S(1)}, f32[42,1,258]{2,0,1:T(8,128)S(1)}, u32[]{:S(2)}, u32[]{:S(2)}) %collective-permute-start.19) | collective-permute-done | bytes 43376 | tf_op jit(solution)/shard_map/ppermute | solution.py:18
  254.5 1.4 copy-done.4
  255.9 5.9 %subtract_select_fusion = f32[40,32,256]{2,0,1:T(8,128)} fusion(pred[40,32,256]{2,0,1:T(8,128)(4,1)S(1)} %get-tuple-element.55, f32[40,32,256]{2,0,1:T(8,128)S(1)} %copy-done.38, f32[42,34,258]{2,0,1:T(8,128)S(1)} %maximum_select_fusion.3, f32[40,32,256]{2,0,1:T(8,128)S(1)} %copy-done.34, f32[40,32,256]{2,0,1:T(8,128)S(1)} %copy-done.30, ...), kind=kLoop, calls=%fused_computation.9 | loop fusion | flops 13434880 | bytes 21299200 | tf_op jit(solution)/shard_map/jit(_where)/select_n | solution.py:67
  261.9 18.2 %scatter.19 = f32[42,34,258]{2,0,1:T(8,128)} dynamic-update-slice(f32[42,34,258]{2,0,1:T(8,128)} %copy-done.4, f32[40,32,256]{2,0,1:T(8,128)} %subtract_select_fusion, s32[]{:T(128)} %constant.184.clone.1, s32[]{:T(128)} %constant.184.clone.1, s32[]{:T(128)} %constant.184.clone.1) | dynamic-update-slice | bytes 2621444 | tf_op jit(solution)/shard_map/scatter | solution.py:70
  280.0 1.2 fusion.150
  281.2 1.3 collective-permute-start.20
  282.5 1.3 collective-permute-start.21
  283.8 1.9 slice.502
  285.8 2.7 collective-permute-done.21
  288.5 2.2 collective-permute-start.22
  290.8 1.6 collective-permute-start.23
  292.7 6.1 %collective-permute-done.23 = f32[42,1,258]{2,0,1:T(8,128)S(1)} collective-permute-done((f32[42,1,258]{2,0,1:T(8,128)S(1)}, f32[42,1,258]{2,0,1:T(8,128)S(1)}, u32[]{:S(2)}, u32[]{:S(2)}) %collective-permute-start.23) | collective-permute-done | bytes 43376 | tf_op jit(solution)/shard_map/ppermute | solution.py:18
  300.0 5.4 %fusion.100 = f32[]{:T(128)} fusion(f32[40,32,256]{2,0,1:T(8,128)S(1)} %copy-done.39, f32[42,34,258]{2,0,1:T(8,128)S(1)} %maximum_select_fusion.4, f32[40,32,256]{2,0,1:T(8,128)S(1)} %copy-done.35, f32[40,32,256]{2,0,1:T(8,128)S(1)} %copy-done.31, f32[40,32,256]{2,0,1:T(8,128)S(1)} %copy-done.27, f32[40,32,256]{2,0,1:T(8,128)S(1)} %copy-done.23, ...), kind=kLoop, calls=%fused_computation.170 | loop fusion | flops 10485759 | bytes 19660804 | tf_op jit(solution)/shard_map/reduce_sum | solution.py:136
  305.3 1.5 copy.14
  306.8 8.4 %psum.7 = f32[]{:T(128)} all-reduce(f32[]{:T(128)} %fusion.100), channel_id=1, replica_groups=mesh['box'=32,'sx'=2,'sy'=2] {'sx','sy'}, use_global_device_ids=true, to_apply=%region_1.2 | all-reduce | flops 1 | bytes 8 | tf_op jit(solution)/shard_map/psum | solution.py:137
  (134 shorter events, 10.0 us)
Async XLA Ops:
  7.2 8.6 %copy-start = (s32[32,3]{0,1:T(4,128)S(1)}, s32[32,3]{0,1:T(4,128)}, u32[]{:S(2)}) copy-start(s32[32,3]{0,1:T(4,128)} %param.14) | copy-start | bytes 1156
  7.2 66.9 %all-gather.2.cloned.1.call-start = ((), (), s32[]{:S(2)}) async-start(), calls=%async_computation | async-start | bytes 12976128 | tf_op jit(solution)/shard_map/all_gather | solution.py:88
  10.0 13.1 %copy-start.40 = (f32[1,40,32,256]{3,1,2,0:T(8,128)}, f32[1,40,32,256]{3,1,2,0:T(8,128)S(1)}, u32[]{:S(2)}) copy-start(f32[1,40,32,256]{3,1,2,0:T(8,128)S(1)} %copy.49) | copy-start | bytes 3932164
  11.1 87.0 %collective-permute-start.5 = (f32[1,32,258]{2,0,1:T(1,128)}, f32[1,32,258]{2,0,1:T(1,128)S(1)}, u32[]{:S(2)}, u32[]{:S(2)}) collective-permute-start(f32[1,32,258]{2,0,1:T(1,128)} %get-tuple-element.86), channel_id=1, source_target_pairs={{0,2},{1,3},{4,6},{5,7},{8,10},{9,11},{12,14},{13,15},{16,18},{17,... | collective-permute-start | bytes 99080 | tf_op jit(solution)/shard_map/ppermute | solution.py:15
  14.5 83.6 %collective-permute-start.4 = (f32[1,32,258]{2,0,1:T(1,128)S(1)}, f32[1,32,258]{2,0,1:T(1,128)S(1)}, u32[]{:S(2)}, u32[]{:S(2)}) collective-permute-start(f32[1,32,258]{2,0,1:T(1,128)S(1)} %get-tuple-element.87), channel_id=1, source_target_pairs={{2,0},{3,1},{6,4},{7,5},{10,8},{11,9},{14,12},{15,13},{18,16},{19,... | collective-permute-start | bytes 99080 | tf_op jit(solution)/shard_map/ppermute | solution.py:18
  82.7 5.5 %collective-permute-start = (f32[1,32,258]{2,0,1:T(1,128)S(1)}, f32[1,32,258]{2,0,1:T(1,128)S(1)}, u32[]{:S(2)}, u32[]{:S(2)}) collective-permute-start(f32[1,32,258]{2,0,1:T(1,128)S(1)} %get-tuple-element.72), channel_id=1, source_target_pairs={{0,2},{1,3},{4,6},{5,7},{8,10},{9,11},{12,14},{13,15},{16,18},{17,... | collective-permute-start | bytes 99080 | tf_op jit(solution)/shard_map/ppermute | solution.py:15
  86.1 6.0 %collective-permute-start.1 = (f32[1,32,258]{2,0,1:T(1,128)S(1)}, f32[1,32,258]{2,0,1:T(1,128)S(1)}, u32[]{:S(2)}, u32[]{:S(2)}) collective-permute-start(f32[1,32,258]{2,0,1:T(1,128)S(1)} %get-tuple-element.73), channel_id=1, source_target_pairs={{2,0},{3,1},{6,4},{7,5},{10,8},{11,9},{14,12},{15,13},{18,16},{19,... | collective-permute-start | bytes 99080 | tf_op jit(solution)/shard_map/ppermute | solution.py:18
  92.1 14.4 %collective-permute-start.2 = (f32[42,1,258]{2,0,1:T(8,128)S(1)}, f32[42,1,258]{2,0,1:T(8,128)S(1)}, u32[]{:S(2)}, u32[]{:S(2)}) collective-permute-start(f32[42,1,258]{2,0,1:T(8,128)S(1)} %get-tuple-element.84), channel_id=1, source_target_pairs={{0,1},{2,3},{4,5},{6,7},{8,9},{10,11},{12,13},{14,15},{16,17},{18,... | collective-permute-start | bytes 130040 | tf_op jit(solution)/shard_map/ppermute | solution.py:15
  96.7 9.8 %collective-permute-start.3 = (f32[42,1,258]{2,0,1:T(8,128)S(1)}, f32[42,1,258]{2,0,1:T(8,128)S(1)}, u32[]{:S(2)}, u32[]{:S(2)}) collective-permute-start(f32[42,1,258]{2,0,1:T(8,128)S(1)} %get-tuple-element.85), channel_id=1, source_target_pairs={{1,0},{3,2},{5,4},{7,6},{9,8},{11,10},{13,12},{15,14},{17,16},{19,... | collective-permute-start | bytes 130040 | tf_op jit(solution)/shard_map/ppermute | solution.py:18
  98.1 9.5 %collective-permute-start.7 = (f32[42,1,258]{2,0,1:T(8,128)S(1)}, f32[42,1,258]{2,0,1:T(8,128)}, u32[]{:S(2)}, u32[]{:S(2)}) collective-permute-start(f32[42,1,258]{2,0,1:T(8,128)S(1)} %get-tuple-element.82), channel_id=1, source_target_pairs={{0,1},{2,3},{4,5},{6,7},{8,9},{10,11},{12,13},{14,15},{16,17},{18,... | collective-permute-start | bytes 130040 | tf_op jit(solution)/shard_map/ppermute | solution.py:15
  104.8 8.1 %copy-start.11 = (f32[1,40,32,256]{3,2,1,0:T(8,128)S(1)}, f32[1,40,32,256]{3,2,1,0:T(8,128)}, u32[]{:S(2)}) copy-start(f32[1,40,32,256]{3,2,1,0:T(8,128)} %param.16) | copy-start | bytes 3932164
  104.8 8.1 %collective-permute-start.6 = (f32[42,1,258]{2,0,1:T(8,128)S(1)}, f32[42,1,258]{2,0,1:T(8,128)}, u32[]{:S(2)}, u32[]{:S(2)}) collective-permute-start(f32[42,1,258]{2,0,1:T(8,128)S(1)} %get-tuple-element.83), channel_id=1, source_target_pairs={{1,0},{3,2},{5,4},{7,6},{9,8},{11,10},{13,12},{15,14},{17,16},{19,... | collective-permute-start | bytes 130040 | tf_op jit(solution)/shard_map/ppermute | solution.py:18
  107.6 18.3 %copy-start.2 = (f32[42,34,258]{2,0,1:T(8,128)}, f32[42,34,258]{2,0,1:T(8,128)S(1)}, u32[]{:S(2)}) copy-start(f32[42,34,258]{2,0,1:T(8,128)S(1)} %maximum_select_fusion) | copy-start | bytes 4421092
  145.3 4.6 %collective-permute-start.8 = (f32[1,32,258]{2,0,1:T(1,128)S(1)}, f32[1,32,258]{2,0,1:T(1,128)S(1)}, u32[]{:S(2)}, u32[]{:S(2)}) collective-permute-start(f32[1,32,258]{2,0,1:T(1,128)S(1)} %get-tuple-element.70), channel_id=1, source_target_pairs={{0,2},{1,3},{4,6},{5,7},{8,10},{9,11},{12,14},{13,15},{16,18},{17,... | collective-permute-start | bytes 99080 | tf_op jit(solution)/shard_map/ppermute | solution.py:15
  146.6 6.2 %collective-permute-start.9 = (f32[1,32,258]{2,0,1:T(1,128)S(1)}, f32[1,32,258]{2,0,1:T(1,128)S(1)}, u32[]{:S(2)}, u32[]{:S(2)}) collective-permute-start(f32[1,32,258]{2,0,1:T(1,128)S(1)} %get-tuple-element.71), channel_id=1, source_target_pairs={{2,0},{3,1},{6,4},{7,5},{10,8},{11,9},{14,12},{15,13},{18,16},{19,... | collective-permute-start | bytes 99080 | tf_op jit(solution)/shard_map/ppermute | solution.py:18
  147.9 16.3 %copy-start.36 = (f32[40,32,256]{2,0,1:T(8,128)S(1)}, f32[40,32,256]{2,0,1:T(8,128)}, u32[]{:S(2)}) copy-start(f32[40,32,256]{2,0,1:T(8,128)} %get-tuple-element.63) | copy-start | bytes 3932164
  147.9 16.3 %copy-start.43 = (s32[42,34,256]{2,0,1:T(8,128)S(1)}, s32[42,34,256]{2,0,1:T(8,128)}, u32[]{:S(2)}) copy-start(s32[42,34,256]{2,0,1:T(8,128)} %negate_select_fusion) | copy-start | bytes 4386820
  152.8 11.5 %copy-start.28 = (f32[40,32,256]{2,0,1:T(8,128)S(1)}, f32[40,32,256]{2,0,1:T(8,128)}, u32[]{:S(2)}) copy-start(f32[40,32,256]{2,0,1:T(8,128)} %get-tuple-element.60) | copy-start | bytes 3932164
  152.8 11.5 %copy-start.32 = (f32[40,32,256]{2,0,1:T(8,128)S(1)}, f32[40,32,256]{2,0,1:T(8,128)}, u32[]{:S(2)}) copy-start(f32[40,32,256]{2,0,1:T(8,128)} %get-tuple-element.61) | copy-start | bytes 3932164
  152.8 4.3 %collective-permute-start.10 = (f32[42,1,258]{2,0,1:T(8,128)S(1)}, f32[42,1,258]{2,0,1:T(8,128)S(1)}, u32[]{:S(2)}, u32[]{:S(2)}) collective-permute-start(f32[42,1,258]{2,0,1:T(8,128)S(1)} %get-tuple-element.80), channel_id=1, source_target_pairs={{0,1},{2,3},{4,5},{6,7},{8,9},{10,11},{12,13},{14,15},{16,17},{18,... | collective-permute-start | bytes 130040 | tf_op jit(solution)/shard_map/ppermute | solution.py:15
  155.1 9.2 %copy-start.7 = (f32[1,40,32,256]{3,2,1,0:T(8,128)S(1)}, f32[1,40,32,256]{3,2,1,0:T(8,128)}, u32[]{:S(2)}) copy-start(f32[1,40,32,256]{3,2,1,0:T(8,128)} %param.17) | copy-start | bytes 3932164
  155.1 9.1 %copy-start.12 = (f32[1,40,32,256]{3,2,1,0:T(8,128)S(1)}, f32[1,40,32,256]{3,2,1,0:T(8,128)}, u32[]{:S(2)}) copy-start(f32[1,40,32,256]{3,2,1,0:T(8,128)} %param.16) | copy-start | bytes 3932164
  155.1 9.1 %copy-start.16 = (f32[40,32,256]{2,0,1:T(8,128)S(1)}, f32[40,32,256]{2,0,1:T(8,128)}, u32[]{:S(2)}) copy-start(f32[40,32,256]{2,0,1:T(8,128)} %get-tuple-element.57) | copy-start | bytes 3932164
  155.1 9.1 %copy-start.20 = (f32[40,32,256]{2,0,1:T(8,128)S(1)}, f32[40,32,256]{2,0,1:T(8,128)}, u32[]{:S(2)}) copy-start(f32[40,32,256]{2,0,1:T(8,128)} %get-tuple-element.58) | copy-start | bytes 3932164
  155.1 9.1 %copy-start.24 = (f32[40,32,256]{2,0,1:T(8,128)S(1)}, f32[40,32,256]{2,0,1:T(8,128)}, u32[]{:S(2)}) copy-start(f32[40,32,256]{2,0,1:T(8,128)} %get-tuple-element.59) | copy-start | bytes 3932164
  155.1 8.0 %collective-permute-start.11 = (f32[42,1,258]{2,0,1:T(8,128)S(1)}, f32[42,1,258]{2,0,1:T(8,128)S(1)}, u32[]{:S(2)}, u32[]{:S(2)}) collective-permute-start(f32[42,1,258]{2,0,1:T(8,128)S(1)} %get-tuple-element.81), channel_id=1, source_target_pairs={{1,0},{3,2},{5,4},{7,6},{9,8},{11,10},{13,12},{15,14},{17,16},{19,... | collective-permute-start | bytes 130040 | tf_op jit(solution)/shard_map/ppermute | solution.py:18
  190.3 4.6 %collective-permute-start.12 = (f32[1,32,258]{2,0,1:T(1,128)S(1)}, f32[1,32,258]{2,0,1:T(1,128)S(1)}, u32[]{:S(2)}, u32[]{:S(2)}) collective-permute-start(f32[1,32,258]{2,0,1:T(1,128)S(1)} %get-tuple-element.68), channel_id=1, source_target_pairs={{0,2},{1,3},{4,6},{5,7},{8,10},{9,11},{12,14},{13,15},{16,18},{17,... | collective-permute-start | bytes 99080 | tf_op jit(solution)/shard_map/ppermute | solution.py:15
  191.6 6.0 %collective-permute-start.13 = (f32[1,32,258]{2,0,1:T(1,128)S(1)}, f32[1,32,258]{2,0,1:T(1,128)S(1)}, u32[]{:S(2)}, u32[]{:S(2)}) collective-permute-start(f32[1,32,258]{2,0,1:T(1,128)S(1)} %get-tuple-element.69), channel_id=1, source_target_pairs={{2,0},{3,1},{6,4},{7,5},{10,8},{11,9},{14,12},{15,13},{18,16},{19,... | collective-permute-start | bytes 99080 | tf_op jit(solution)/shard_map/ppermute | solution.py:18
  192.9 17.6 %copy-start.37 = (f32[40,32,256]{2,0,1:T(8,128)S(1)}, f32[40,32,256]{2,0,1:T(8,128)}, u32[]{:S(2)}) copy-start(f32[40,32,256]{2,0,1:T(8,128)} %get-tuple-element.63) | copy-start | bytes 3932164
  192.9 17.6 %copy-start.44 = (pred[40,32,256]{2,0,1:T(8,128)(4,1)S(1)}, pred[40,32,256]{2,0,1:T(8,128)(4,1)}, u32[]{:S(2)}) copy-start(pred[40,32,256]{2,0,1:T(8,128)(4,1)} %get-tuple-element.62) | copy-start | bytes 983044
  197.5 12.9 %copy-start.29 = (f32[40,32,256]{2,0,1:T(8,128)S(1)}, f32[40,32,256]{2,0,1:T(8,128)}, u32[]{:S(2)}) copy-start(f32[40,32,256]{2,0,1:T(8,128)} %get-tuple-element.60) | copy-start | bytes 3932164
  197.5 12.9 %copy-start.33 = (f32[40,32,256]{2,0,1:T(8,128)S(1)}, f32[40,32,256]{2,0,1:T(8,128)}, u32[]{:S(2)}) copy-start(f32[40,32,256]{2,0,1:T(8,128)} %get-tuple-element.61) | copy-start | bytes 3932164
  197.6 4.3 %collective-permute-start.14 = (f32[42,1,258]{2,0,1:T(8,128)S(1)}, f32[42,1,258]{2,0,1:T(8,128)S(1)}, u32[]{:S(2)}, u32[]{:S(2)}) collective-permute-start(f32[42,1,258]{2,0,1:T(8,128)S(1)} %get-tuple-element.78), channel_id=1, source_target_pairs={{0,1},{2,3},{4,5},{6,7},{8,9},{10,11},{12,13},{14,15},{16,17},{18,... | collective-permute-start | bytes 130040 | tf_op jit(solution)/shard_map/ppermute | solution.py:15
  199.9 10.6 %copy-start.8 = (f32[1,40,32,256]{3,2,1,0:T(8,128)S(1)}, f32[1,40,32,256]{3,2,1,0:T(8,128)}, u32[]{:S(2)}) copy-start(f32[1,40,32,256]{3,2,1,0:T(8,128)} %param.17) | copy-start | bytes 3932164
  199.9 10.6 %copy-start.13 = (f32[1,40,32,256]{3,2,1,0:T(8,128)S(1)}, f32[1,40,32,256]{3,2,1,0:T(8,128)}, u32[]{:S(2)}) copy-start(f32[1,40,32,256]{3,2,1,0:T(8,128)} %param.16) | copy-start | bytes 3932164
  199.9 10.6 %copy-start.17 = (f32[40,32,256]{2,0,1:T(8,128)S(1)}, f32[40,32,256]{2,0,1:T(8,128)}, u32[]{:S(2)}) copy-start(f32[40,32,256]{2,0,1:T(8,128)} %get-tuple-element.57) | copy-start | bytes 3932164
  199.9 10.6 %copy-start.21 = (f32[40,32,256]{2,0,1:T(8,128)S(1)}, f32[40,32,256]{2,0,1:T(8,128)}, u32[]{:S(2)}) copy-start(f32[40,32,256]{2,0,1:T(8,128)} %get-tuple-element.58) | copy-start | bytes 3932164
  199.9 10.6 %copy-start.25 = (f32[40,32,256]{2,0,1:T(8,128)S(1)}, f32[40,32,256]{2,0,1:T(8,128)}, u32[]{:S(2)}) copy-start(f32[40,32,256]{2,0,1:T(8,128)} %get-tuple-element.59) | copy-start | bytes 3932164
  199.9 8.0 %collective-permute-start.15 = (f32[42,1,258]{2,0,1:T(8,128)S(1)}, f32[42,1,258]{2,0,1:T(8,128)S(1)}, u32[]{:S(2)}, u32[]{:S(2)}) collective-permute-start(f32[42,1,258]{2,0,1:T(8,128)S(1)} %get-tuple-element.79), channel_id=1, source_target_pairs={{1,0},{3,2},{5,4},{7,6},{9,8},{11,10},{13,12},{15,14},{17,16},{19,... | collective-permute-start | bytes 130040 | tf_op jit(solution)/shard_map/ppermute | solution.py:18
  235.8 4.5 %collective-permute-start.16 = (f32[1,32,258]{2,0,1:T(1,128)S(1)}, f32[1,32,258]{2,0,1:T(1,128)S(1)}, u32[]{:S(2)}, u32[]{:S(2)}) collective-permute-start(f32[1,32,258]{2,0,1:T(1,128)S(1)} %get-tuple-element.66), channel_id=1, source_target_pairs={{0,2},{1,3},{4,6},{5,7},{8,10},{9,11},{12,14},{13,15},{16,18},{17,... | collective-permute-start | bytes 99080 | tf_op jit(solution)/shard_map/ppermute | solution.py:15
  237.1 6.0 %collective-permute-start.17 = (f32[1,32,258]{2,0,1:T(1,128)S(1)}, f32[1,32,258]{2,0,1:T(1,128)S(1)}, u32[]{:S(2)}, u32[]{:S(2)}) collective-permute-start(f32[1,32,258]{2,0,1:T(1,128)S(1)} %get-tuple-element.67), channel_id=1, source_target_pairs={{2,0},{3,1},{6,4},{7,5},{10,8},{11,9},{14,12},{15,13},{18,16},{19,... | collective-permute-start | bytes 99080 | tf_op jit(solution)/shard_map/ppermute | solution.py:18
  238.4 17.5 %copy-start.38 = (f32[40,32,256]{2,0,1:T(8,128)S(1)}, f32[40,32,256]{2,0,1:T(8,128)}, u32[]{:S(2)}) copy-start(f32[40,32,256]{2,0,1:T(8,128)} %get-tuple-element.63) | copy-start | bytes 3932164
  243.0 12.8 %copy-start.30 = (f32[40,32,256]{2,0,1:T(8,128)S(1)}, f32[40,32,256]{2,0,1:T(8,128)}, u32[]{:S(2)}) copy-start(f32[40,32,256]{2,0,1:T(8,128)} %get-tuple-element.60) | copy-start | bytes 3932164
  243.0 12.8 %copy-start.34 = (f32[40,32,256]{2,0,1:T(8,128)S(1)}, f32[40,32,256]{2,0,1:T(8,128)}, u32[]{:S(2)}) copy-start(f32[40,32,256]{2,0,1:T(8,128)} %get-tuple-element.61) | copy-start | bytes 3932164
  243.1 4.2 %collective-permute-start.18 = (f32[42,1,258]{2,0,1:T(8,128)S(1)}, f32[42,1,258]{2,0,1:T(8,128)S(1)}, u32[]{:S(2)}, u32[]{:S(2)}) collective-permute-start(f32[42,1,258]{2,0,1:T(8,128)S(1)} %get-tuple-element.76), channel_id=1, source_target_pairs={{0,1},{2,3},{4,5},{6,7},{8,9},{10,11},{12,13},{14,15},{16,17},{18,... | collective-permute-start | bytes 130040 | tf_op jit(solution)/shard_map/ppermute | solution.py:15
  245.3 10.6 %copy-start.9 = (f32[1,40,32,256]{3,2,1,0:T(8,128)S(1)}, f32[1,40,32,256]{3,2,1,0:T(8,128)}, u32[]{:S(2)}) copy-start(f32[1,40,32,256]{3,2,1,0:T(8,128)} %param.17) | copy-start | bytes 3932164
  245.4 10.5 %copy-start.14 = (f32[1,40,32,256]{3,2,1,0:T(8,128)S(1)}, f32[1,40,32,256]{3,2,1,0:T(8,128)}, u32[]{:S(2)}) copy-start(f32[1,40,32,256]{3,2,1,0:T(8,128)} %param.16) | copy-start | bytes 3932164
  245.4 10.5 %copy-start.18 = (f32[40,32,256]{2,0,1:T(8,128)S(1)}, f32[40,32,256]{2,0,1:T(8,128)}, u32[]{:S(2)}) copy-start(f32[40,32,256]{2,0,1:T(8,128)} %get-tuple-element.57) | copy-start | bytes 3932164
  245.4 10.5 %copy-start.22 = (f32[40,32,256]{2,0,1:T(8,128)S(1)}, f32[40,32,256]{2,0,1:T(8,128)}, u32[]{:S(2)}) copy-start(f32[40,32,256]{2,0,1:T(8,128)} %get-tuple-element.58) | copy-start | bytes 3932164
  245.4 10.5 %copy-start.26 = (f32[40,32,256]{2,0,1:T(8,128)S(1)}, f32[40,32,256]{2,0,1:T(8,128)}, u32[]{:S(2)}) copy-start(f32[40,32,256]{2,0,1:T(8,128)} %get-tuple-element.59) | copy-start | bytes 3932164
  245.4 8.0 %collective-permute-start.19 = (f32[42,1,258]{2,0,1:T(8,128)S(1)}, f32[42,1,258]{2,0,1:T(8,128)S(1)}, u32[]{:S(2)}, u32[]{:S(2)}) collective-permute-start(f32[42,1,258]{2,0,1:T(8,128)S(1)} %get-tuple-element.77), channel_id=1, source_target_pairs={{1,0},{3,2},{5,4},{7,6},{9,8},{11,10},{13,12},{15,14},{17,16},{19,... | collective-permute-start | bytes 130040 | tf_op jit(solution)/shard_map/ppermute | solution.py:18
  281.2 4.5 %collective-permute-start.20 = (f32[1,32,258]{2,0,1:T(1,128)S(1)}, f32[1,32,258]{2,0,1:T(1,128)S(1)}, u32[]{:S(2)}, u32[]{:S(2)}) collective-permute-start(f32[1,32,258]{2,0,1:T(1,128)S(1)} %get-tuple-element.64), channel_id=1, source_target_pairs={{0,2},{1,3},{4,6},{5,7},{8,10},{9,11},{12,14},{13,15},{16,18},{17,... | collective-permute-start | bytes 99080 | tf_op jit(solution)/shard_map/ppermute | solution.py:15
  282.5 6.0 %collective-permute-start.21 = (f32[1,32,258]{2,0,1:T(1,128)S(1)}, f32[1,32,258]{2,0,1:T(1,128)S(1)}, u32[]{:S(2)}, u32[]{:S(2)}) collective-permute-start(f32[1,32,258]{2,0,1:T(1,128)S(1)} %get-tuple-element.65), channel_id=1, source_target_pairs={{2,0},{3,1},{6,4},{7,5},{10,8},{11,9},{14,12},{15,13},{18,16},{19,... | collective-permute-start | bytes 99080 | tf_op jit(solution)/shard_map/ppermute | solution.py:18
  283.8 16.1 %copy-start.39 = (f32[40,32,256]{2,0,1:T(8,128)S(1)}, f32[40,32,256]{2,0,1:T(8,128)}, u32[]{:S(2)}) copy-start(f32[40,32,256]{2,0,1:T(8,128)} %get-tuple-element.63) | copy-start | bytes 3932164
  288.5 11.4 %copy-start.31 = (f32[40,32,256]{2,0,1:T(8,128)S(1)}, f32[40,32,256]{2,0,1:T(8,128)}, u32[]{:S(2)}) copy-start(f32[40,32,256]{2,0,1:T(8,128)} %get-tuple-element.60) | copy-start | bytes 3932164
  288.5 11.4 %copy-start.35 = (f32[40,32,256]{2,0,1:T(8,128)S(1)}, f32[40,32,256]{2,0,1:T(8,128)}, u32[]{:S(2)}) copy-start(f32[40,32,256]{2,0,1:T(8,128)} %get-tuple-element.61) | copy-start | bytes 3932164
  288.5 4.2 %collective-permute-start.22 = (f32[42,1,258]{2,0,1:T(8,128)S(1)}, f32[42,1,258]{2,0,1:T(8,128)S(1)}, u32[]{:S(2)}, u32[]{:S(2)}) collective-permute-start(f32[42,1,258]{2,0,1:T(8,128)S(1)} %get-tuple-element.74), channel_id=1, source_target_pairs={{0,1},{2,3},{4,5},{6,7},{8,9},{10,11},{12,13},{14,15},{16,17},{18,... | collective-permute-start | bytes 130040 | tf_op jit(solution)/shard_map/ppermute | solution.py:15
  290.8 9.1 %copy-start.10 = (f32[1,40,32,256]{3,2,1,0:T(8,128)S(1)}, f32[1,40,32,256]{3,2,1,0:T(8,128)}, u32[]{:S(2)}) copy-start(f32[1,40,32,256]{3,2,1,0:T(8,128)} %param.17) | copy-start | bytes 3932164
  290.8 9.1 %copy-start.15 = (f32[1,40,32,256]{3,2,1,0:T(8,128)S(1)}, f32[1,40,32,256]{3,2,1,0:T(8,128)}, u32[]{:S(2)}) copy-start(f32[1,40,32,256]{3,2,1,0:T(8,128)} %param.16) | copy-start | bytes 3932164
  290.8 9.1 %copy-start.19 = (f32[40,32,256]{2,0,1:T(8,128)S(1)}, f32[40,32,256]{2,0,1:T(8,128)}, u32[]{:S(2)}) copy-start(f32[40,32,256]{2,0,1:T(8,128)} %get-tuple-element.57) | copy-start | bytes 3932164
  290.8 9.1 %copy-start.23 = (f32[40,32,256]{2,0,1:T(8,128)S(1)}, f32[40,32,256]{2,0,1:T(8,128)}, u32[]{:S(2)}) copy-start(f32[40,32,256]{2,0,1:T(8,128)} %get-tuple-element.58) | copy-start | bytes 3932164
  290.8 9.1 %copy-start.27 = (f32[40,32,256]{2,0,1:T(8,128)S(1)}, f32[40,32,256]{2,0,1:T(8,128)}, u32[]{:S(2)}) copy-start(f32[40,32,256]{2,0,1:T(8,128)} %get-tuple-element.59) | copy-start | bytes 3932164
  290.8 8.0 %collective-permute-start.23 = (f32[42,1,258]{2,0,1:T(8,128)S(1)}, f32[42,1,258]{2,0,1:T(8,128)S(1)}, u32[]{:S(2)}, u32[]{:S(2)}) collective-permute-start(f32[42,1,258]{2,0,1:T(8,128)S(1)} %get-tuple-element.75), channel_id=1, source_target_pairs={{1,0},{3,2},{5,4},{7,6},{9,8},{11,10},{13,12},{15,14},{17,16},{19,... | collective-permute-start | bytes 130040 | tf_op jit(solution)/shard_map/ppermute | solution.py:18
  305.3 10.5 %copy-start.1 = (s32[32,3]{0,1:T(4,128)S(1)}, s32[32,3]{0,1:T(4,128)}, u32[]{:S(2)}) copy-start(s32[32,3]{0,1:T(4,128)} %param.14) | copy-start | bytes 1156
  (6 other events, 30.1 us)
Sparse Core Ops, SparseCore 0:
  10.3 63.7 all-gather.1
where the time goes:
time: 329 us; the launch traced here: 324 us
  waiting for transfers between devices  97.5 us (30%)
  local copies, waits for them, and re-layouts  97.3 us (30%)
  starting transfers between devices  49.5 us (15%)
  other arithmetic  44.9 us (14%)
  between operations  20.8 us (6%)
  blocking collectives  8.37 us (3%)
  matrix products  5.44 us (2%)
    scatter x4, local copies, waits for them, and re-layouts, smooth(): return values.at[1:-1, 1:-1, 1:-1].set(updated)  72.7 us
    all_gather x1, waiting for transfers between devices, body(): portion = lax.all_gather(coarse, 'box', axis=0, tiled=True)  51 us
    ppermute x12, waiting for transfers between devices, padded_2(): lax.ppermute(lax.slice_in_dim(block, 0, width, axis=dim), axis, backward)  44.7 us
    ppermute x12, starting transfers between devices, padded_2(): lax.ppermute(lax.slice_in_dim(block, block.shape[dim] - width, None, axis...  32.3 us
    select_n x4, other arithmetic, smooth(): jnp.where(active, centre - residual / (weights + screening * jnp.cosh(cen...  31.5 us
    ppermute x12, starting transfers between devices, padded_2(): lax.ppermute(lax.slice_in_dim(block, 0, width, axis=dim), axis, backward)  17.2 us
    psum x1, blocking collectives, body(): group_total = lax.psum(own_squares, ('sx', 'sy'))  8.37 us
    slice x4, local copies, waits for them, and re-layouts, body(): potential = padded[1:-1, 1:-1]  7.72 us
  transfers between devices with their start and end apart: 25, of which 15 were waited for; matrix products, arithmetic and copies ran while one was open for 8% of the time, Pallas kernels for 0%

commit v1 on v0

v1 whole, which is shorter than its diff:
```python
import functools

import jax
import jax.numpy as jnp
from jax import lax
from jax.experimental import pallas as pl
from jax.experimental.pallas import tpu as pltpu
from jax.sharding import PartitionSpec as P

RATIO = 4
LOG2E = 1.4426950408889634
MESH = pl.DeviceIdType.MESH
F32 = jnp.float32


def iota(shape, dim):
    return lax.broadcasted_iota(jnp.int32, shape, dim)


def kernel(
    boxes, tx, ty, cells,
    anchors, coarse, diel, screen, source,
    pot_out, norm_out,
    slab, packed, arrived, zin, zfine, ylines, xlines,
    raw_e, raw_k, raw_s, eps, scr, chg, w, diag, u, pot,
    xsend, xrecv, ysend, yrecv, sums,
    slab_sem, raw_sem, pot_sem, pack_send, pack_recv,
    xs_sem, xr_sem, ys_sem, yr_sem, ss_sem, sr_sem,
):
    pairs = tx // 2
    nrows = (tx + 1) // RATIO + 2
    ncols = (ty + 1) // RATIO + 2
    slabs = slab.shape[1]
    deep = zin.shape[0] // ncols
    lines = ylines.shape[1] // (ty + 16)
    top = 8 + ty
    me = lax.axis_index("box")
    sx = lax.axis_index("sx")
    sy = lax.axis_index("sy")
    group = 2 * sx + sy
    peers = [{"sx": 1 - sx}, {"sy": 1 - sy}, {"sx": 1 - sx, "sy": 1 - sy}]

    barrier = pltpu.get_barrier_semaphore()

    def greet(d, _):
        pl.semaphore_signal(
            barrier, inc=1, device_id={"box": lax.rem(me + d, boxes)}, device_id_type=MESH
        )
        return 0

    lax.fori_loop(1, boxes, greet, 0)
    for peer in peers:
        pl.semaphore_signal(barrier, inc=1, device_id=peer, device_id_type=MESH)

    slab_in = [
        pltpu.make_async_copy(coarse.at[r], slab.at[:, r, :], slab_sem.at[r]) for r in range(slabs)
    ]
    raw_in = [
        pltpu.make_async_copy(src.at[0], dst, raw_sem.at[n])
        for n, (src, dst) in enumerate(((diel, raw_e), (screen, raw_k), (source, raw_s)))
    ]
    for copy in slab_in + raw_in:
        copy.start()
    for copy in slab_in:
        copy.wait()
    pl.semaphore_wait(barrier, boxes - 1 + 3)

    lane8 = iota((8, 128), 1)

    def window(d):
        b = lax.rem(me + d, boxes)
        y0 = anchors[b, 1] + sy * (ty // RATIO)
        z0 = anchors[b, 2]
        to_even = lax.rem(128 - z0, 128)
        to_odd = lax.rem(192 - z0, 128)
        parts = []
        extra = jnp.zeros((8, 128), F32)
        for m in range(ncols // 2):
            even = pltpu.roll(slab[y0 + 2 * m], to_even, 1)
            odd = pltpu.roll(slab[y0 + 2 * m + 1], to_odd, 1)
            parts.append(jnp.where(lane8 < 64, even, odd))
            ends = jnp.where(lane8 < 64, odd, even)
            if m > 0:
                ends = pltpu.roll(ends, 2 * m, 1)
            extra = jnp.where((lane8 % 64) // 2 == m, ends, extra)
        return parts + [extra]

    def send_window(d, _):
        for m, part in enumerate(window(d)):
            packed[d, m] = part
        pltpu.make_async_remote_copy(
            src_ref=packed.at[d],
            dst_ref=arrived.at[d],
            send_sem=pack_send,
            recv_sem=pack_recv,
            device_id={"box": lax.rem(me + d, boxes)},
            device_id_type=MESH,
        ).start()
        return 0

    lax.fori_loop(1, boxes, send_window, 0)
    for m, part in enumerate(window(0)):
        arrived[0, m] = part

    odd_tile = (iota((ty, 128), 0) + iota((ty, 128), 1)) % 2 == 1
    odd_tall = (iota((ty + 16, 128), 0) + iota((ty + 16, 128), 1)) % 2 == 1
    lane = iota((ty, 128), 1)

    def split(ref, k, h):
        low = ref[2 * k, :, pl.ds(128 * h, 128)]
        high = ref[2 * k + 1, :, pl.ds(128 * h, 128)]
        return jnp.where(odd_tile, high, low), jnp.where(odd_tile, low, high)

    def x_copy(slot):
        return pltpu.make_async_remote_copy(
            src_ref=xsend.at[slot], dst_ref=xrecv.at[slot],
            send_sem=xs_sem.at[slot], recv_sem=xr_sem.at[slot],
            device_id=peers[0], device_id_type=MESH,
        )

    def y_copy(slot):
        return pltpu.make_async_remote_copy(
            src_ref=ysend.at[slot], dst_ref=yrecv.at[slot],
            send_sem=ys_sem.at[slot], recv_sem=yr_sem.at[slot],
            device_id=peers[1], device_id_type=MESH,
        )

    x_edge = pairs - (pairs - 1) * sx
    x_halo = (pairs + 1) * (1 - sx)
    y_edge = top - 1 - (ty - 1) * sy
    y_halo = top - (ty + 1) * sy

    def send_halo(ref, colour, slot):
        for h in range(2):
            xsend[slot, h] = ref[colour, h, x_edge, 8:top, :]
        x_copy(slot).start()
        for h in range(2):
            for k in range(pairs):
                ysend[slot, h, k : k + 1, :] = ref[colour, h, k + 1, pl.ds(y_edge, 1), :]
        y_copy(slot).start()

    def take_halo(ref, colour, slot):
        x_copy(slot).wait_recv()
        for h in range(2):
            ref[colour, h, x_halo, 8:top, :] = xrecv[slot, h]
        y_copy(slot).wait_recv()
        for h in range(2):
            for k in range(pairs):
                ref[colour, h, k + 1, pl.ds(y_halo, 1), :] = yrecv[slot, h, k : k + 1, :]

    def around(ref, colour, kk):
        other = 1 - colour
        b = [ref[other, h, kk, 8:top, :] for h in range(2)]
        ends = ref[colour, 2, kk, 8:top, :]
        up = [pltpu.roll(v, 1, 1) for v in b]
        down = [pltpu.roll(v, 127, 1) for v in b]
        below = [jnp.where(lane == 0, ends, up[0]), jnp.where(lane == 0, up[0], up[1])]
        above = [jnp.where(lane == 127, down[1], down[0]), jnp.where(lane == 127, ends, down[1])]
        result = []
        for h in range(2):
            before = ref[other, h, kk - 1, 8:top, :]
            after = ref[other, h, kk + 1, 8:top, :]
            if colour == 0:
                outer = jnp.where(odd_tile, after, before)
            else:
                outer = jnp.where(odd_tile, before, after)
            result.append((
                b[h], outer,
                ref[other, h, kk, 7 : top - 1, :], ref[other, h, kk, 9 : top + 1, :],
                below[h], above[h],
            ))
        return result

    zero_tall = jnp.zeros((ty + 16, 128), F32)

    def clear(kk, _):
        for colour in range(2):
            for h in range(3):
                eps[colour, h, kk] = zero_tall
        return 0

    lax.fori_loop(0, pairs + 2, clear, 0)
    raw_in[0].wait()

    def split_eps(k, _):
        for h in range(2):
            red, black = split(raw_e, k, h)
            eps[0, h, k + 1, 8:top, :] = red
            eps[1, h, k + 1, 8:top, :] = black
        return 0

    lax.fori_loop(0, pairs, split_eps, 0)
    for colour in range(2):
        send_halo(eps, colour, colour)
    raw_in[1].wait()
    raw_in[2].wait()

    def split_rest(k, _):
        for h in range(2):
            for src, dst in ((raw_k, scr), (raw_s, chg)):
                red, black = split(src, k, h)
                dst[0, h, k] = red
                dst[1, h, k] = black
        return 0

    lax.fori_loop(0, pairs, split_rest, 0)
    for colour in range(2):
        take_halo(eps, colour, colour)

    def couple(k, _):
        for colour in range(2):
            near = around(eps, colour, k + 1)
            for h in range(2):
                own = eps[colour, h, k + 1, 8:top, :]
                total = None
                for n in range(6):
                    weight = 0.5 * (own + near[h][n])
                    w[colour, n, h, k] = weight
                    total = weight if total is None else total + weight
                diag[colour, h, k] = total
        return 0

    lax.fori_loop(0, pairs, couple, 0)

    row = iota((128, 128), 0)
    col = iota((128, 128), 1)
    pz = []
    for h in range(3):
        if h < 2:
            q = col + 128 * h + 1
        else:
            q = jnp.where(col == 0, 0, 257)
        low = q // RATIO
        part = (q - low * RATIO).astype(F32) / RATIO
        pz.append(
            (jnp.where(row == low, 1.0 - part, 0.0) + jnp.where(row == low + 1, part, 0.0)).astype(jnp.bfloat16)
        )

    pltpu.make_async_copy(arrived.at[pl.ds(1, boxes - 1)], arrived.at[pl.ds(1, boxes - 1)], pack_recv).wait()
    row0 = anchors[me, 0] + sx * (tx // RATIO)
    first = row0 // 8
    phase = row0 - first * 8
    for t in range(deep // 8):
        holder = jnp.minimum(first + t, boxes - 1)
        slot = lax.rem(me - holder + boxes, boxes)
        extra = arrived[slot, ncols // 2]
        for m in range(ncols // 2):
            part = arrived[slot, m]
            ends = pltpu.roll(extra, 128 - 2 * m, 1) if m > 0 else extra
            even = jnp.where(lane8 < 64, part, ends)
            odd = pltpu.roll(jnp.where(lane8 < 64, ends, part), 64, 1)
            zin[pl.ds((2 * m) * deep + 8 * t, 8), :] = even
            zin[pl.ds((2 * m + 1) * deep + 8 * t, 8), :] = odd
    values = zin[...]
    split_parts = []
    for _ in range(3):
        part = values.astype(jnp.bfloat16)
        split_parts.append(part)
        values = values - part.astype(F32)
    for h in range(3):
        zfine[h] = sum(jnp.dot(part, pz[h], preferred_element_type=F32) for part in reversed(split_parts))

    for h in range(3):
        columns = [zfine[h, pl.ds(c * deep + phase, lines), :] for c in range(ncols)]
        for q in range(ty + 2):
            low, part = q // RATIO, (q % RATIO) / RATIO
            value = columns[low]
            if part > 0:
                value = (1.0 - part) * value + part * columns[low + 1]
            ylines[h, pl.ds((q + 7) * lines, lines), :] = value
    for h in range(3):
        for r in range(nrows):
            xlines[h, r] = ylines[h, pl.ds(r, ty + 16, stride=lines), :]

    def guess(m, _):
        for h in range(3):
            before = xlines[h, jnp.maximum(m - 1, 0)]
            here = xlines[h, m]
            after = xlines[h, m + 1]
            planes = (
                (2 * m, 0.25 * before + 0.75 * here, here),
                (2 * m + 1, 0.75 * here + 0.25 * after, 0.5 * here + 0.5 * after),
            )
            for kk, low, high in planes:
                u[0, h, kk] = jnp.where(odd_tall, high, low)
                u[1, h, kk] = jnp.where(odd_tall, low, high)
        return 0

    lax.fori_loop(0, tx // RATIO + 1, guess, 0)

    def near_sum(colour, k):
        near = around(u, colour, k + 1)
        result = []
        for h in range(2):
            total = None
            for n in range(6):
                term = w[colour, n, h, k] * near[h][n]
                total = term if total is None else total + term
            result.append(total)
        return result

    def hyperbolic(value):
        power = value * LOG2E
        plus = jnp.exp2(power - 1.0)
        minus = jnp.exp2(-1.0 - power)
        return plus - minus, plus + minus

    def half_sweep(colour, last):
        def step(k, acc):
            pulls = near_sum(colour, k)
            for h in range(2):
                centre = u[colour, h, k + 1, 8:top, :]
                main = diag[colour, h, k]
                salt = scr[colour, h, k]
                pull = pulls[h] + chg[colour, h, k]
                sinh, cosh = hyperbolic(centre)
                g = main * centre - pull + salt * sinh
                d = main + salt * cosh
                value = centre - g / d
                u[colour, h, k + 1, 8:top, :] = value
                if last:
                    g = main * value - pull + salt * hyperbolic(value)[0]
                    acc = acc + g * g
            return acc

        if last:
            return lax.fori_loop(0, pairs, step, jnp.zeros((ty, 128), F32))
        lax.fori_loop(0, pairs, lambda k, c: step(k, c), 0)
        return None

    for turn in range(4):
        colour = turn % 2
        total = half_sweep(colour, turn == 3)
        send_halo(u, colour, 2 + turn)
        if turn < 3:
            take_halo(u, colour, 2 + turn)

    def join(k, _):
        for h in range(2):
            red = u[0, h, k + 1, 8:top, :]
            black = u[1, h, k + 1, 8:top, :]
            pot[2 * k, :, pl.ds(128 * h, 128)] = jnp.where(odd_tile, black, red)
            pot[2 * k + 1, :, pl.ds(128 * h, 128)] = jnp.where(odd_tile, red, black)
        return 0

    lax.fori_loop(0, pairs, join, 0)
    pot_copy = pltpu.make_async_copy(pot, pot_out.at[0], pot_sem)
    pot_copy.start()
    take_halo(u, 1, 5)

    def remainder(k, acc):
        pulls = near_sum(0, k)
        for h in range(2):
            centre = u[0, h, k + 1, 8:top, :]
            pull = pulls[h] + chg[0, h, k]
            g = diag[0, h, k] * centre - pull + scr[0, h, k] * hyperbolic(centre)[0]
            acc = acc + g * g
        return acc

    total = lax.fori_loop(0, pairs, remainder, total)
    part = total[0:8]
    for t in range(1, ty // 8):
        part = part + total[8 * t : 8 * t + 8]
    sums[group] = part
    sum_copies = [
        pltpu.make_async_remote_copy(
            src_ref=sums.at[group], dst_ref=sums.at[group],
            send_sem=ss_sem.at[n], recv_sem=sr_sem.at[n],
            device_id=peer, device_id_type=MESH,
        )
        for n, peer in enumerate(peers)
    ]
    for copy in sum_copies:
        copy.start()

    pltpu.make_async_copy(packed.at[pl.ds(1, boxes - 1)], packed.at[pl.ds(1, boxes - 1)], pack_send).wait()
    for slot in range(6):
        x_copy(slot).wait_send()
        y_copy(slot).wait_send()
    for copy in sum_copies:
        copy.wait()
    squares = jnp.sum(sums[0] + sums[1] + sums[2] + sums[3], keepdims=True)
    norm_out[...] = jnp.sqrt(squares / cells + 1e-06)
    pot_copy.wait()


def body(coarse, anchors, dielectric, screening, source):
    boxes = lax.axis_size("box")
    _, tx, ty, tz = dielectric.shape
    pairs = tx // 2
    nrows = (tx + 1) // RATIO + 2
    ncols = (ty + 1) // RATIO + 2
    deep = (nrows + 14) // 8 * 8
    lines = (nrows + 7) // 8 * 8
    slabs, gy, gz = coarse.shape
    cells = tx * ty * tz * lax.axis_size("sx") * lax.axis_size("sy")
    any_spec = pl.BlockSpec(memory_space=pl.ANY)
    dma = pltpu.SemaphoreType.DMA

    def vmem(*shape):
        return pltpu.VMEM(shape, F32)

    potential, norm = pl.pallas_call(
        functools.partial(kernel, boxes, tx, ty, cells),
        out_shape=(
            jax.ShapeDtypeStruct((1, tx, ty, tz), F32),
            jax.ShapeDtypeStruct((1, 1), F32),
        ),
        in_specs=[pl.BlockSpec(memory_space=pltpu.SMEM)] + [any_spec] * 4,
        out_specs=(any_spec, pl.BlockSpec(memory_space=pltpu.VMEM)),
        scratch_shapes=[
            vmem(gy, slabs, gz),
            vmem(boxes, ncols // 2 + 1, 8, 128),
            vmem(boxes, ncols // 2 + 1, 8, 128),
            vmem(ncols * deep, 128),
            vmem(3, ncols * deep, 128),
            vmem(3, (ty + 16) * lines, 128),
            vmem(3, nrows, ty + 16, 128),
            vmem(tx, ty, tz),
            vmem(tx, ty, tz),
            vmem(tx, ty, tz),
            vmem(2, 3, pairs + 2, ty + 16, 128),
            vmem(2, 2, pairs, ty, 128),
            vmem(2, 2, pairs, ty, 128),
            vmem(2, 6, 2, pairs, ty, 128),
            vmem(2, 2, pairs, ty, 128),
            vmem(2, 3, pairs + 2, ty + 16, 128),
            vmem(tx, ty, tz),
            vmem(6, 2, ty, 128),
            vmem(6, 2, ty, 128),
            vmem(6, 2, pairs, 128),
            vmem(6, 2, pairs, 128),
            vmem(4, 8, 128),
            dma((slabs,)), dma((3,)), dma, dma, dma,
            dma((6,)), dma((6,)), dma((6,)), dma((6,)), dma((3,)), dma((3,)),
        ],
        compiler_params=pltpu.CompilerParams(
            collective_id=0, has_side_effects=True, vmem_limit_bytes=56 * 1024 * 1024
        ),
        cost_estimate=pl.CostEstimate(
            flops=200 * tx * ty * tz, bytes_accessed=16 * tx * ty * tz, transcendentals=12 * tx * ty * tz
        ),
    )(anchors, coarse, dielectric, screening, source)
    return potential, norm.reshape(1)


def solution(mesh):
    tile = P("box", "sx", "sy", None)
    return jax.shard_map(
        body,
        mesh=mesh,
        in_specs=(P("box", None, None), P(), tile, tile, tile),
        out_specs=(tile, P("box")),
        check_vma=False,
    )
```

time: 329 us -> 60.4 us (0.18); the launches traced: 324 us -> 59.7 us
  waiting for transfers between devices: 97.5 us -> 0 us
  local copies, waits for them, and re-layouts: 97.3 us -> 3.89 us
  Pallas kernels: 0 us -> 53.4 us
  starting transfers between devices: 49.5 us -> 0 us
  other arithmetic: 44.9 us -> 0 us
  between operations: 20.8 us -> 2.39 us
  blocking collectives: 8.37 us -> 0 us
  matrix products: 5.44 us -> 0 us
    scatter x4 -> x0, local copies, waits for them, and re-layouts: 72.7 us -> none  [smooth(): return values.at[1:-1, 1:-1, 1:-1].set(updated)]
    pallas_call x0 -> x1, Pallas kernels: none -> 53.4 us  [body(): pl.pallas_call(functools.partial(kernel, boxes, tx, ty, cells), out_shape...]
    all_gather x1 -> x0, waiting for transfers between devices: 51 us -> none  [body(): portion = lax.all_gather(coarse, 'box', axis=0, tiled=True)]
    ppermute x24 -> x0, starting transfers between devices: 49.5 us -> none  [the longest x12 32.3 us: padded_2(): lax.ppermute(lax.slice_in_dim(block, block.shape[dim] - width, None, axis...]
    ppermute x24 -> x0, waiting for transfers between devices: 45.8 us -> none  [the longest x12 44.7 us: padded_2(): lax.ppermute(lax.slice_in_dim(block, 0, width, axis=dim), axis, backward)]
    select_n x9 -> x0, other arithmetic: 36.7 us -> none  [the longest x4 31.5 us: smooth(): jnp.where(active, centre - residual / (weights + screening * jnp.cosh(cen...]
    slice x12 -> x0, local copies, waits for them, and re-layouts: 14.3 us -> none  [the longest x4 7.72 us: body(): potential = padded[1:-1, 1:-1]]
    psum x1 -> x0, blocking collectives: 8.37 us -> none  [body(): group_total = lax.psum(own_squares, ('sx', 'sy'))]
  transfers between devices with their start and end apart: 25 -> 0, of which waited for: 15 -> 0; matrix products, arithmetic and copies ran while one was open for 8% -> 0% of each run, Pallas kernels for 0% -> 0%
where the time goes in v1:
time: 60.4 us; the launch traced here: 59.7 us
  Pallas kernels  53.4 us (88%)
  local copies, waits for them, and re-layouts  3.89 us (6%)
  between operations  2.39 us (4%)
    pallas_call x1, Pallas kernels, body(): pl.pallas_call(functools.partial(kernel, boxes, tx, ty, cells), out_shape...  53.4 us
    unnamed x2, local copies, waits for them, and re-layouts  3.89 us

profile of v1, /device:TPU:96, one launch (start us, length us, event | category | flops | bytes accessed | tf_op | source)
XLA Modules:
  0.0 59.7 jit_solution(17706727005098735256)
XLA Ops:
  0.6 1.4 %copy.7.anchors = s32[32,3]{1,0:T(8,128)} copy(s32[32,3]{0,1:T(4,128)} %param.6) | data formatting | bytes 768 | tf_op args[1]
  2.0 53.4 %shard_map.68 = (f32[1,40,32,256]{3,2,1,0:T(8,128)}, f32[1,1]{1,0:T(1,128)}) custom-call(s32[32,3]{1,0:T(8,128)} %copy.7.anchors, f32[8,96,128]{2,1,0:T(8,128)} %coarse.1, f32[1,40,32,256]{3,2,1,0:T(8,128)} %diel.1, f32[1,40,32,256]{3,2,1,0:T(8,128)} %screen.1, f32[1,40,32,256]{3,2,1,0:T(8,128)} %source.1), custom_call_target="tpu_custom_call" | custom-call | flops 65536000 | bytes 5242880 | tf_op jit(solution)/shard_map/pallas_call | solution.py:403
  55.4 2.5 %copy.10 = f32[1,40,32,256]{3,2,1,0:T(8,128)} copy(f32[1,40,32,256]{3,2,1,0:T(8,128)} %get-tuple-element.8) | data formatting | bytes 2621440

commit v2 on v1

v2 whole, which is shorter than its diff:
```python
import functools

import jax
import jax.numpy as jnp
from jax import lax
from jax.experimental import pallas as pl
from jax.experimental.pallas import tpu as pltpu
from jax.sharding import PartitionSpec as P

RATIO = 4
LOG2E = 1.4426950408889634
MESH = pl.DeviceIdType.MESH
F32 = jnp.float32


def iota(shape, dim):
    return lax.broadcasted_iota(jnp.int32, shape, dim)


def loop(count, step, carry, unroll):
    chunks = count // unroll if count > unroll else 0

    def chunk(n, carry):
        for i in range(unroll):
            carry = step(n * unroll + i, carry)
        return carry

    if chunks:
        carry = lax.fori_loop(0, chunks, chunk, carry)
    for i in range(chunks * unroll, count):
        carry = step(i, carry)
    return carry


def kernel(
    boxes, tx, ty, cells,
    anchors_in, coarse, diel, screen, source,
    pot, norm_out,
    anchors, slab, packed, arrived, zin, zfine, ylines, xlines,
    raw_e, raw_k, raw_s, er, eb, scr, chg, w, diag, ur, ub, uend,
    wx, dx, wy, dy, line_r, line_b, line_end,
    sxs, sxr, sys, syr, sds, sdr, dxs, dxr, dys, dyr, dds, ddr, sums,
    anchor_sem, slab_sem, raw_sem, pack_send, pack_recv, halo_send, halo_recv, ss_sem, sr_sem,
):
    pairs = tx // 2
    nrows = (tx + 1) // RATIO + 2
    ncols = (ty + 1) // RATIO + 2
    slabs = slab.shape[1]
    deep = zin.shape[0] // ncols
    lines = ylines.shape[1] // (ty + 16)
    top = 8 + ty
    me = lax.axis_index("box")
    sx = lax.axis_index("sx")
    sy = lax.axis_index("sy")
    group = 2 * sx + sy
    peers = [{"sx": 1 - sx}, {"sy": 1 - sy}, {"sx": 1 - sx, "sy": 1 - sy}]

    x_edge = pairs - (pairs - 1) * sx
    x_halo = (pairs + 1) * (1 - sx)
    x_far = (pairs + 1) * sx
    y_edge = top - 1 - (ty - 1) * sy
    y_next = y_edge - 1 + 2 * sy
    y_halo = top - (ty + 1) * sy

    anchor_in = pltpu.make_async_copy(anchors_in, anchors, anchor_sem)
    slab_in = [
        pltpu.make_async_copy(coarse.at[r], slab.at[:, r, :], slab_sem.at[r]) for r in range(slabs)
    ]
    raw_in = [
        pltpu.make_async_copy(src.at[0], dst, raw_sem.at[n])
        for n, (src, dst) in enumerate(((diel, raw_e), (screen, raw_k), (source, raw_s)))
    ]
    anchor_in.start()
    for copy in slab_in:
        copy.start()

    barrier = pltpu.get_barrier_semaphore()

    def greet(d, _):
        pl.semaphore_signal(
            barrier, inc=1, device_id={"box": lax.rem(me + d, boxes)}, device_id_type=MESH
        )
        return 0

    lax.fori_loop(1, boxes, greet, 0)
    for peer in peers:
        pl.semaphore_signal(barrier, inc=1, device_id=peer, device_id_type=MESH)
    for copy in raw_in:
        copy.start()

    lane8 = iota((8, 128), 1)

    def window(d):
        b = lax.rem(me + d, boxes)
        y0 = anchors[1, b] + sy * (ty // RATIO)
        z0 = anchors[2, b]
        to_even = lax.rem(128 - z0, 128)
        to_odd = lax.rem(192 - z0, 128)
        parts = []
        extra = jnp.zeros((8, 128), F32)
        for m in range(ncols // 2):
            even = pltpu.roll(slab[y0 + 2 * m], to_even, 1)
            odd = pltpu.roll(slab[y0 + 2 * m + 1], to_odd, 1)
            parts.append(jnp.where(lane8 < 64, even, odd))
            ends = jnp.where(lane8 < 64, odd, even)
            if m > 0:
                ends = pltpu.roll(ends, 2 * m, 1)
            extra = jnp.where((lane8 % 64) // 2 == m, ends, extra)
        return parts + [extra]

    def pack_window(d, _):
        for m, part in enumerate(window(d + 1)):
            packed[d + 1, m] = part
        return 0

    def send_window(d, _):
        pltpu.make_async_remote_copy(
            src_ref=packed.at[d],
            dst_ref=arrived.at[d],
            send_sem=pack_send,
            recv_sem=pack_recv,
            device_id={"box": lax.rem(me + d, boxes)},
            device_id_type=MESH,
        ).start()
        return 0

    anchor_in.wait()
    for copy in slab_in:
        copy.wait()
    loop(boxes - 1, pack_window, 0, 4)
    pl.semaphore_wait(barrier, boxes - 1 + 3)
    lax.fori_loop(1, boxes, send_window, 0)
    for m, part in enumerate(window(0)):
        arrived[0, m] = part

    odd_tile = (iota((ty, 128), 0) + iota((ty, 128), 1)) % 2 == 1
    odd_tall = (iota((ty + 16, 128), 0) + iota((ty + 16, 128), 1)) % 2 == 1
    odd8 = (iota((8, 128), 0) + iota((8, 128), 1)) % 2 == 1
    odd_line = (iota((pairs, 128), 1) + y_halo) % 2 == 1

    halo_src = [[sxs, sys, sds]] + [[dxs.at[t], dys.at[t], dds.at[t]] for t in range(2)]
    halo_dst = [[sxr, syr, sdr]] + [[dxr.at[t], dyr.at[t], ddr.at[t]] for t in range(2)]

    def halo_copies(slot):
        return [
            pltpu.make_async_remote_copy(
                src_ref=halo_src[slot][n], dst_ref=halo_dst[slot][n],
                send_sem=halo_send.at[3 * slot + n], recv_sem=halo_recv.at[3 * slot + n],
                device_id=peers[n], device_id_type=MESH,
            )
            for n in range(3)
        ]

    def around(ref, ends, colour, kk, r0, rows, odd, outer=None):
        lane = iota((rows, 128), 1)
        here = pl.ds(r0 + 8, rows)
        b = [ref[h, kk, here, :] for h in range(2)]
        below, above = along_z(b, ends, lane)
        result = []
        for h in range(2):
            if outer is None:
                before = ref[h, kk - 1, here, :]
                after = ref[h, kk + 1, here, :]
                side = jnp.where(odd, after, before) if colour == 0 else jnp.where(odd, before, after)
            else:
                side = ref[h, outer, here, :]
            result.append([
                b[h], side, ref[h, kk, pl.ds(r0 + 7, rows), :], ref[h, kk, pl.ds(r0 + 9, rows), :],
                below[h], above[h],
            ])
        return result

    def along_z(b, ends, lane):
        up = [pltpu.roll(v, 1, 1) for v in b]
        down = [pltpu.roll(v, 127, 1) for v in b]
        below = [jnp.where(lane == 0, ends, up[0]), jnp.where(lane == 0, up[0], up[1])]
        above = [jnp.where(lane == 127, down[1], down[0]), jnp.where(lane == 127, ends, down[1])]
        return below, above

    def around_line(own_edge, far, ends):
        b = [line_r[h, pl.ds(1, pairs), :] for h in range(2)]
        below, above = along_z(b, ends, iota((pairs, 128), 1))
        result = []
        for h in range(2):
            before = line_r[h, pl.ds(0, pairs), :]
            after = line_r[h, pl.ds(2, pairs), :]
            side = jnp.where(odd_line, before, after)
            result.append([b[h], side, own_edge[h], far[h], below[h], above[h]])
        return result

    def rows_to(dst, ref, row, first):
        for h in range(2):
            for k in range(pairs):
                dst[h, k : k + 1, :] = ref[h, k + first, pl.ds(row, 1), :]

    def rows_from(src, ref):
        for h in range(2):
            for k in range(pairs):
                ref[h, k + 1, pl.ds(y_halo, 1), :] = src[h, k : k + 1, :]

    def corner_to(dst, ref):
        for h in range(2):
            dst[h : h + 1, :] = ref[h, x_edge, pl.ds(y_edge, 1), :]

    def take_red(ref, xr, yr, dr, outside):
        for h in range(2):
            ref[h, x_halo, 8:top, :] = xr[h]
            ref[h, x_halo, pl.ds(y_halo, 1), :] = dr[h : h + 1, :]
            line_r[h, pl.ds(1, pairs), :] = yr[h]
            line_r[h, pl.ds(x_halo, 1), :] = dr[h : h + 1, :]
            line_r[h, pl.ds(x_far, 1), :] = outside[h]
        rows_from(yr, ref)

    zero_tall = jnp.zeros((ty + 16, 128), F32)

    def clear(kk, _):
        for h in range(2):
            er[h, kk] = zero_tall
            eb[h, kk] = zero_tall
        return 0

    lax.fori_loop(0, pairs + 2, clear, 0)
    sds[...] = jnp.zeros((8, 128), F32)
    for t in range(2):
        dds[t] = jnp.zeros((8, 128), F32)

    def split(ref, k, h):
        low = ref[2 * k, :, pl.ds(128 * h, 128)]
        high = ref[2 * k + 1, :, pl.ds(128 * h, 128)]
        return jnp.where(odd_tile, high, low), jnp.where(odd_tile, low, high)

    def split_eps(k, _):
        for h in range(2):
            er[h, k + 1, 8:top, :], eb[h, k + 1, 8:top, :] = split(raw_e, k, h)
        return 0

    def split_rest(k, _):
        for h in range(2):
            for src, dst in ((raw_k, scr), (raw_s, chg)):
                dst[0, h, k], dst[1, h, k] = split(src, k, h)
        return 0

    raw_in[0].wait()
    loop(pairs, split_eps, 0, 2)
    raw_in[1].wait()
    raw_in[2].wait()
    loop(pairs, split_rest, 0, 2)
    for h in range(2):
        sxs[0, h] = er[h, x_edge, 8:top, :]
        sxs[1, h] = eb[h, x_edge, 8:top, :]
        sxs[2, h] = scr[1, h, x_edge - 1]
        sxs[3, h] = chg[1, h, x_edge - 1]
    rows_to(sys.at[0], er, y_edge, 1)
    rows_to(sys.at[1], er, y_next, 1)
    rows_to(sys.at[2], eb, y_edge, 1)
    rows_to(sys.at[3], scr.at[1], y_edge - 8, 0)
    rows_to(sys.at[4], chg.at[1], y_edge - 8, 0)
    corner_to(sds, er)
    for copy in halo_copies(0):
        copy.start()
    for copy in halo_copies(0):
        copy.wait_recv()
    zero_line = jnp.zeros((1, 128), F32)
    take_red(er, sxr.at[0], syr.at[0], sdr, (zero_line, zero_line))
    for h in range(2):
        eb[h, x_halo, 8:top, :] = sxr[1, h]
    rows_from(syr.at[2], eb)

    def weigh(own, near):
        weights = [0.5 * (own + value) for value in near]
        return weights, sum(weights[1:], weights[0])

    def couple(k, _):
        for colour, mine, other in ((0, er, eb), (1, eb, er)):
            near = around(other, 0.0, colour, k + 1, 0, ty, odd_tile)
            for h in range(2):
                weights, total = weigh(mine[h, k + 1, 8:top, :], near[h])
                for n in range(6):
                    w[colour, n, h, k] = weights[n]
                diag[colour, h, k] = total
        return 0

    loop(pairs, couple, 0, 2)
    near_x = around(er, 0.0, 1, x_halo, 0, ty, odd_tile, x_edge)
    near_y = around_line(sys[0], syr[1], 0.0)
    for h in range(2):
        weights, dx[h] = weigh(eb[h, x_halo, 8:top, :], near_x[h])
        for n in range(6):
            wx[n, h] = weights[n]
        weights, dy[h] = weigh(syr[2, h], near_y[h])
        for n in range(6):
            wy[n, h] = weights[n]

    row = iota((128, 128), 0)
    col = iota((128, 128), 1)
    pz = []
    for h in range(3):
        if h < 2:
            q = col + 128 * h + 1
        else:
            q = jnp.where(col == 0, 0, 257)
        low = q // RATIO
        part = (q - low * RATIO).astype(F32) / RATIO
        pz.append(
            (jnp.where(row == low, 1.0 - part, 0.0) + jnp.where(row == low + 1, part, 0.0)).astype(jnp.bfloat16)
        )

    pltpu.make_async_copy(arrived.at[pl.ds(1, boxes - 1)], arrived.at[pl.ds(1, boxes - 1)], pack_recv).wait()
    row0 = anchors[0, me] + sx * (tx // RATIO)
    first = row0 // 8
    phase = row0 - first * 8
    for t in range(deep // 8):
        holder = jnp.minimum(first + t, boxes - 1)
        slot = lax.rem(me - holder + boxes, boxes)
        extra = arrived[slot, ncols // 2]
        for m in range(ncols // 2):
            part = arrived[slot, m]
            ends = pltpu.roll(extra, 128 - 2 * m, 1) if m > 0 else extra
            even = jnp.where(lane8 < 64, part, ends)
            odd = pltpu.roll(jnp.where(lane8 < 64, ends, part), 64, 1)
            zin[pl.ds((2 * m) * deep + 8 * t, 8), :] = even
            zin[pl.ds((2 * m + 1) * deep + 8 * t, 8), :] = odd
    values = zin[...]
    split_parts = []
    for _ in range(3):
        part = values.astype(jnp.bfloat16)
        split_parts.append(part)
        values = values - part.astype(F32)
    for h in range(3):
        zfine[h] = sum(jnp.dot(part, pz[h], preferred_element_type=F32) for part in reversed(split_parts))

    for h in range(3):
        columns = [zfine[h, pl.ds(c * deep + phase, lines), :] for c in range(ncols)]
        for q in range(ty + 2):
            low, part = q // RATIO, (q % RATIO) / RATIO
            value = columns[low]
            if part > 0:
                value = (1.0 - part) * value + part * columns[low + 1]
            ylines[h, pl.ds((q + 7) * lines, lines), :] = value
    for h in range(3):
        for r in range(nrows):
            xlines[h, r] = ylines[h, pl.ds(r, ty + 16, stride=lines), :]

    def guess(m, _):
        for h in range(3):
            before = xlines[h, jnp.maximum(m - 1, 0)]
            here = xlines[h, m]
            after = xlines[h, m + 1]
            planes = (
                (2 * m, 0.25 * before + 0.75 * here, here),
                (2 * m + 1, 0.75 * here + 0.25 * after, 0.5 * here + 0.5 * after),
            )
            for kk, low, high in planes:
                red = jnp.where(odd_tall, high, low)
                black = jnp.where(odd_tall, low, high)
                if h < 2:
                    ur[h, kk] = red
                    ub[h, kk] = black
                else:
                    uend[0, kk] = red
                    uend[1, kk] = black
        return 0

    loop(tx // RATIO + 1, guess, 0, 2)

    def hyperbolic(value):
        power = value * LOG2E
        plus = jnp.exp2(power - 1.0)
        minus = jnp.exp2(-1.0 - power)
        return plus - minus, plus + minus

    def weighted(weights, near):
        total = weights(0) * near[0]
        for n in (4, 5, 1, 2, 3):
            total = total + weights(n) * near[n]
        return total

    def newton(centre, pull, main, salt):
        sinh, cosh = hyperbolic(centre)
        return centre - (main * centre - pull + salt * sinh) / (main + salt * cosh)

    def square(centre, pull, main, salt):
        g = main * centre - pull + salt * hyperbolic(centre)[0]
        return g * g

    def cells_of(colour, kk, r0, acc, update, residual):
        here = pl.ds(r0, 8)
        own, other = (ur, ub) if colour == 0 else (ub, ur)
        k = kk - 1
        near = around(other, uend[colour, kk, pl.ds(r0 + 8, 8), :], colour, kk, r0, 8, odd8)
        for h in range(2):
            pull = weighted(lambda n: w[colour, n, h, k, here, :], near[h]) + chg[colour, h, k, here, :]
            main = diag[colour, h, k, here, :]
            salt = scr[colour, h, k, here, :]
            value = own[h, kk, pl.ds(r0 + 8, 8), :]
            if update:
                value = newton(value, pull, main, salt)
                own[h, kk, pl.ds(r0 + 8, 8), :] = value
            if residual:
                acc = acc + square(value, pull, main, salt)
        return acc

    inner_pair = 1 + sx
    inner_row = pl.multiple_of(8 * sy, 8)
    edge_row = pl.multiple_of((ty - 8) * (1 - sy), 8)

    def edge(colour, acc, residual):
        for r0 in range(0, ty, 8):
            acc = cells_of(colour, x_edge, r0, acc, True, residual)
        return loop(
            pairs - 1,
            lambda i, acc: cells_of(colour, inner_pair + i, edge_row, acc, True, residual),
            acc, pairs,
        )

    def interior(colour, acc, residual):
        def step(i, acc):
            for s in range(ty // 8 - 1):
                acc = cells_of(colour, inner_pair + i, pl.multiple_of(inner_row + 8 * s, 8), acc, True, residual)
            return acc

        return loop(pairs - 1, step, acc, 5)

    def send_red(t):
        for h in range(2):
            dxs[t, h] = ur[h, x_edge, 8:top, :]
        rows_to(dys.at[t, 0], ur, y_edge, 1)
        rows_to(dys.at[t, 1], ur, y_next, 1)
        corner_to(dds.at[t], ur)
        for copy in halo_copies(1 + t):
            copy.start()

    def take(t):
        for copy in halo_copies(1 + t):
            copy.wait_recv()
        outside = [ur[h, x_far, pl.ds(y_halo, 1), :] for h in range(2)]
        take_red(ur, dxr.at[t], dyr.at[t, 0], ddr.at[t], outside)

    def beside(t):
        near_x = around(ur, uend[1, x_halo, 8:top, :], 1, x_halo, 0, ty, odd_tile, x_edge)
        near_y = around_line(dys[t, 0], dyr[t, 1], line_end[...])
        for h in range(2):
            pull = weighted(lambda n: wx[n, h], near_x[h]) + sxr[3, h]
            ub[h, x_halo, 8:top, :] = newton(ub[h, x_halo, 8:top, :], pull, dx[h], sxr[2, h])
            pull = weighted(lambda n: wy[n, h], near_y[h]) + syr[4, h]
            line_b[h] = newton(line_b[h], pull, dy[h], syr[3, h])
        rows_from(line_b, ub)

    rows_to(line_b, ub, y_halo, 1)
    for k in range(pairs):
        line_end[k : k + 1, :] = uend[1, k + 1, pl.ds(y_halo, 1), :]
    total = jnp.zeros((8, 128), F32)
    for t in range(2):
        edge(0, total, False)
        send_red(t)
        interior(0, total, False)
        total = interior(1, total, t == 1)
        take(t)
        beside(t)
        total = edge(1, total, t == 1)

    def remainder(i, acc):
        for r0 in range(0, ty, 8):
            acc = cells_of(0, i + 1, r0, acc, False, True)
        return acc

    sums[group] = loop(pairs, remainder, total, 5)
    sum_copies = [
        pltpu.make_async_remote_copy(
            src_ref=sums.at[group], dst_ref=sums.at[group],
            send_sem=ss_sem.at[n], recv_sem=sr_sem.at[n],
            device_id=peer, device_id_type=MESH,
        )
        for n, peer in enumerate(peers)
    ]
    for copy in sum_copies:
        copy.start()

    def join(k, _):
        for h in range(2):
            red = ur[h, k + 1, 8:top, :]
            black = ub[h, k + 1, 8:top, :]
            pot[0, 2 * k, :, pl.ds(128 * h, 128)] = jnp.where(odd_tile, black, red)
            pot[0, 2 * k + 1, :, pl.ds(128 * h, 128)] = jnp.where(odd_tile, red, black)
        return 0

    loop(pairs, join, 0, 2)

    pltpu.make_async_copy(packed.at[pl.ds(1, boxes - 1)], packed.at[pl.ds(1, boxes - 1)], pack_send).wait()
    for slot in range(3):
        for copy in halo_copies(slot):
            copy.wait_send()
    for copy in sum_copies:
        copy.wait()
    squares = jnp.sum(sums[0] + sums[1] + sums[2] + sums[3], keepdims=True)
    norm_out[...] = jnp.sqrt(squares / cells + 1e-06)


def body(coarse, anchors, dielectric, screening, source):
    boxes = lax.axis_size("box")
    _, tx, ty, tz = dielectric.shape
    pairs = tx // 2
    nrows = (tx + 1) // RATIO + 2
    ncols = (ty + 1) // RATIO + 2
    deep = (nrows + 14) // 8 * 8
    lines = (nrows + 7) // 8 * 8
    slabs, gy, gz = coarse.shape
    cells = tx * ty * tz * lax.axis_size("sx") * lax.axis_size("sy")
    any_spec = pl.BlockSpec(memory_space=pl.ANY)
    vmem_spec = pl.BlockSpec(memory_space=pltpu.VMEM)
    dma = pltpu.SemaphoreType.DMA

    def vmem(*shape):
        return pltpu.VMEM(shape, F32)

    def padded():
        return vmem(2, pairs + 2, ty + 16, 128)

    potential, norm = pl.pallas_call(
        functools.partial(kernel, boxes, tx, ty, cells),
        out_shape=(
            jax.ShapeDtypeStruct((1, tx, ty, tz), F32),
            jax.ShapeDtypeStruct((1, 1), F32),
        ),
        in_specs=[any_spec] * 5,
        out_specs=(vmem_spec, vmem_spec),
        scratch_shapes=[
            pltpu.SMEM((3, boxes), jnp.int32),
            vmem(gy, slabs, gz),
            vmem(boxes, ncols // 2 + 1, 8, 128),
            vmem(boxes, ncols // 2 + 1, 8, 128),
            vmem(ncols * deep, 128),
            vmem(3, ncols * deep, 128),
            vmem(3, (ty + 16) * lines, 128),
            vmem(3, nrows, ty + 16, 128),
            vmem(tx, ty, tz),
            vmem(tx, ty, tz),
            vmem(tx, ty, tz),
            padded(),
            padded(),
            vmem(2, 2, pairs, ty, 128),
            vmem(2, 2, pairs, ty, 128),
            vmem(2, 6, 2, pairs, ty, 128),
            vmem(2, 2, pairs, ty, 128),
            padded(),
            padded(),
            padded(),
            vmem(6, 2, ty, 128),
            vmem(2, ty, 128),
            vmem(6, 2, pairs, 128),
            vmem(2, pairs, 128),
            vmem(2, pairs + 4, 128),
            vmem(2, pairs, 128),
            vmem(pairs, 128),
            vmem(4, 2, ty, 128),
            vmem(4, 2, ty, 128),
            vmem(5, 2, pairs, 128),
            vmem(5, 2, pairs, 128),
            vmem(8, 128),
            vmem(8, 128),
            vmem(2, 2, ty, 128),
            vmem(2, 2, ty, 128),
            vmem(2, 2, 2, pairs, 128),
            vmem(2, 2, 2, pairs, 128),
            vmem(2, 8, 128),
            vmem(2, 8, 128),
            vmem(4, 8, 128),
            dma, dma((slabs,)), dma((3,)), dma, dma, dma((9,)), dma((9,)), dma((3,)), dma((3,)),
        ],
        compiler_params=pltpu.CompilerParams(
            collective_id=0, has_side_effects=True, vmem_limit_bytes=52 * 1024 * 1024
        ),
        cost_estimate=pl.CostEstimate(
            flops=200 * tx * ty * tz, bytes_accessed=16 * tx * ty * tz, transcendentals=12 * tx * ty * tz
        ),
    )(anchors.T, coarse, dielectric, screening, source)
    return potential, norm.reshape(1)


def solution(mesh):
    tile = P("box", "sx", "sy", None)
    return jax.shard_map(
        body,
        mesh=mesh,
        in_specs=(P("box", None, None), P(), tile, tile, tile),
        out_specs=(tile, P("box")),
        check_vma=False,
    )
```

time: 60.4 us -> 42.2 us (0.70)
  Pallas kernels: 53.4 us -> 36.9 us
  local copies, waits for them, and re-layouts: 3.89 us -> 2.73 us
    pallas_call x1, Pallas kernels: 53.4 us -> 36.9 us  [body(): pl.pallas_call(functools.partial(kernel, boxes, tx, ty, cells), out_shape...]
    unnamed x2 -> x5, local copies, waits for them, and re-layouts: 3.89 us -> 2.73 us
where the time goes in v2:
time: 42.2 us; the launch traced here: 42.1 us
  Pallas kernels  36.9 us (87%)
  local copies, waits for them, and re-layouts  2.73 us (6%)
  between operations  2.41 us (6%)
    pallas_call x1, Pallas kernels, body(): pl.pallas_call(functools.partial(kernel, boxes, tx, ty, cells), out_shape...  36.9 us
    unnamed x5, local copies, waits for them, and re-layouts  2.73 us

profile of v2, /device:TPU:96, one launch (start us, length us, event | category | flops | bytes accessed | tf_op | source)
XLA Modules:
  0.0 42.1 jit_solution(10477327280601820744)
XLA Ops:
  0.6 0.0 copy-start
  0.6 1.0 %copy-done = f32[8,96,128]{2,1,0:T(8,128)S(1)} copy-done((f32[8,96,128]{2,1,0:T(8,128)S(1)}, f32[8,96,128]{2,1,0:T(8,128)}, u32[]{:S(2)}) %copy-start) | copy-done | bytes 393240
  1.6 0.0 copy-start.1
  1.6 0.7 %copy-done.1 = s32[32,3]{0,1:T(4,128)S(1)} copy-done((s32[32,3]{0,1:T(4,128)S(1)}, s32[32,3]{0,1:T(4,128)}, u32[]{:S(2)}) %copy-start.1) | copy-done | bytes 408
  2.3 36.9 %shard_map.68 = (f32[1,40,32,256]{3,2,1,0:T(8,128)S(1)}, f32[1,1]{1,0:T(1,128)}) custom-call(s32[3,32]{1,0:T(4,128)S(1)} %bitcast.2, f32[8,96,128]{2,1,0:T(8,128)S(1)} %copy-done, f32[1,40,32,256]{3,2,1,0:T(8,128)} %diel.1, f32[1,40,32,256]{3,2,1,0:T(8,128)} %screen.1, f32[1,40,32,256]{3,2,1,0:T(8,128)} %source.1), custom_call_target="tpu_custom_call" | custom-call | flops 65536000 | bytes 5242880 | tf_op jit(solution)/shard_map/pallas_call | solution.py:519
  39.2 1.1 %copy.9 = f32[1,40,32,256]{3,2,1,0:T(8,128)} copy(f32[1,40,32,256]{3,2,1,0:T(8,128)S(1)} %get-tuple-element.8) | data formatting | bytes 2621440
Async XLA Ops:
  0.6 1.0 %copy-start = (f32[8,96,128]{2,1,0:T(8,128)S(1)}, f32[8,96,128]{2,1,0:T(8,128)}, u32[]{:S(2)}) copy-start(f32[8,96,128]{2,1,0:T(8,128)} %coarse.1) | copy-start | bytes 1179652
  1.6 0.7 %copy-start.1 = (s32[32,3]{0,1:T(4,128)S(1)}, s32[32,3]{0,1:T(4,128)}, u32[]{:S(2)}) copy-start(s32[32,3]{0,1:T(4,128)} %param.6) | copy-start | bytes 1156

commit v3 on v2

--- a/solution.py
+++ b/solution.py
@@ -449,22 +449,38 @@
     rows_to(line_b, ub, y_halo, 1)
     for k in range(pairs):
         line_end[k : k + 1, :] = uend[1, k + 1, pl.ds(y_halo, 1), :]
+
+    tiles = ty // 8
+    rim = min(2, tiles)
+    free_row = pl.multiple_of(16 * sy, 8)
+    rim_row = pl.multiple_of(8 * (tiles - rim) * (1 - sy), 8)
+
+    def residual_free(i, acc):
+        for s in range(tiles - rim):
+            acc = cells_of(0, 1 + 2 * sx + i, pl.multiple_of(free_row + 8 * s, 8), acc, False, True)
+        return acc
+
+    def residual_rim(i, acc):
+        for s in range(rim):
+            acc = cells_of(0, 1 + 2 * sx + i, pl.multiple_of(rim_row + 8 * s, 8), acc, False, True)
+        return acc
+
     total = jnp.zeros((8, 128), F32)
     for t in range(2):
         edge(0, total, False)
         send_red(t)
         interior(0, total, False)
         total = interior(1, total, t == 1)
+        if t == 1:
+            total = loop(pairs - 2, residual_free, total, 6)
         take(t)
         beside(t)
         total = edge(1, total, t == 1)
 
-    def remainder(i, acc):
+    for i in range(2):
         for r0 in range(0, ty, 8):
-            acc = cells_of(0, i + 1, r0, acc, False, True)
-        return acc
-
-    sums[group] = loop(pairs, remainder, total, 5)
+            total = cells_of(0, (pairs - 2) * (1 - sx) + 1 + i, r0, total, False, True)
+    sums[group] = loop(pairs - 2, residual_rim, total, 6)
     sum_copies = [
         pltpu.make_async_remote_copy(
             src_ref=sums.at[group], dst_ref=sums.at[group],
@@ -573,7 +589,10 @@
         cost_estimate=pl.CostEstimate(
             flops=200 * tx * ty * tz, bytes_accessed=16 * tx * ty * tz, transcendentals=12 * tx * ty * tz
         ),
-    )(anchors.T, coarse, dielectric, screening, source)
+    )(*(
+        pltpu.with_memory_space_constraint(operand, pltpu.HBM)
+        for operand in (anchors.T, coarse, dielectric, screening, source)
+    ))
     return potential, norm.reshape(1)
 
 

time: 42.2 us -> 40 us (0.948)
  local copies, waits for them, and re-layouts: 2.73 us -> 1.06 us
  Pallas kernels: 36.9 us -> 36.3 us
    unnamed x5 -> x1, local copies, waits for them, and re-layouts: 2.73 us -> 1.06 us
    pallas_call x1, Pallas kernels: 36.9 us -> 36.3 us  [body(): pl.pallas_call(functools.partial(kernel, boxes, tx, ty, cells), out_shape...]
where the time goes in v3:
time: 40 us; the launch traced here: 39.7 us
  Pallas kernels  36.3 us (91%)
  between operations  2.33 us (6%)
  local copies, waits for them, and re-layouts  1.06 us (3%)
    pallas_call x1, Pallas kernels, body(): pl.pallas_call(functools.partial(kernel, boxes, tx, ty, cells), out_shape...  36.3 us
    unnamed x1, local copies, waits for them, and re-layouts  1.06 us

profile of v3, /device:TPU:96, one launch (start us, length us, event | category | flops | bytes accessed | tf_op | source)
XLA Modules:
  0.0 39.7 jit_solution(13157604724061533369)
XLA Ops:
  0.6 36.3 %shard_map.68 = (f32[1,40,32,256]{3,2,1,0:T(8,128)S(1)}, f32[1,1]{1,0:T(1,128)}) custom-call(s32[3,32]{1,0:T(4,128)} %bitcast.2, f32[8,96,128]{2,1,0:T(8,128)} %coarse.1, f32[1,40,32,256]{3,2,1,0:T(8,128)} %diel.1, f32[1,40,32,256]{3,2,1,0:T(8,128)} %screen.1, f32[1,40,32,256]{3,2,1,0:T(8,128)} %source.1), custom_call_target="tpu_custom_call" | custom-call | flops 65536000 | bytes 5242880 | tf_op jit(solution)/shard_map/pallas_call | solution.py:535
  37.0 1.1 %copy.9 = f32[1,40,32,256]{3,2,1,0:T(8,128)} copy(f32[1,40,32,256]{3,2,1,0:T(8,128)S(1)} %get-tuple-element.8) | data formatting | bytes 2621440

commit v4 on v3

v4 whole, which is shorter than its diff:
```python
import functools

import jax
import jax.numpy as jnp
from jax import lax
from jax.experimental import pallas as pl
from jax.experimental.pallas import tpu as pltpu
from jax.sharding import PartitionSpec as P

RATIO = 4
LOG2E = 1.4426950408889634
MESH = pl.DeviceIdType.MESH
F32 = jnp.float32


def iota(shape, dim):
    return lax.broadcasted_iota(jnp.int32, shape, dim)


def loop(count, step, carry, unroll):
    chunks = count // unroll if count > unroll else 0

    def chunk(n, carry):
        for i in range(unroll):
            carry = step(n * unroll + i, carry)
        return carry

    if chunks:
        carry = lax.fori_loop(0, chunks, chunk, carry)
    for i in range(chunks * unroll, count):
        carry = step(i, carry)
    return carry


def kernel(
    boxes, tx, ty, cells,
    anchors_in, coarse, diel, screen, source,
    pot, norm_out,
    anchors, slab, packed, arrived, zin, zfine, ylines, xlines,
    raw_e, raw_k, raw_s, er, eb, scr, chg, w, diag, ur, ub, uend,
    wx, dx, wl, dl, kl, sl, le, lu, lend,
    sxs, sxr, sys, syr, sds, sdr, dxs, dxr, dys, dyr, dds, ddr, sums,
    anchor_sem, slab_sem, raw_sem, pack_send, pack_recv, halo_send, halo_recv, ss_sem, sr_sem,
):
    pairs = tx // 2
    nrows = xlines.shape[1]
    ncols = ty // RATIO + 3
    both = ncols // 2
    slabs = slab.shape[1]
    deep = zin.shape[0] // ncols
    lines = ylines.shape[1] // (ty + 16)
    top = 8 + ty
    me = lax.axis_index("box")
    sx = lax.axis_index("sx")
    sy = lax.axis_index("sy")
    group = 2 * sx + sy
    peers = [{"sx": 1 - sx}, {"sy": 1 - sy}, {"sx": 1 - sx, "sy": 1 - sy}]

    x_edge = pairs + 1 - (pairs - 1) * sx
    x_next = x_edge - 1 + 2 * sx
    x_halo = pairs + 2 - (pairs + 1) * sx
    x_outer = (pairs + 3) * (1 - sx)
    x_far = 1 + (pairs + 1) * sx
    outward = 1 - 2 * sy
    y_edge = top - 1 - (ty - 1) * sy
    own_pairs = pl.ds(2, pairs)
    line_pairs = pl.ds(1, pairs + 2)

    anchor_in = pltpu.make_async_copy(anchors_in, anchors, anchor_sem)
    slab_in = [
        pltpu.make_async_copy(coarse.at[r], slab.at[:, r, :], slab_sem.at[r]) for r in range(slabs)
    ]
    raw_in = [
        pltpu.make_async_copy(src.at[0], dst, raw_sem.at[n])
        for n, (src, dst) in enumerate(((diel, raw_e), (screen, raw_k), (source, raw_s)))
    ]
    anchor_in.start()
    for copy in slab_in:
        copy.start()

    barrier = pltpu.get_barrier_semaphore()

    def greet(d, _):
        pl.semaphore_signal(
            barrier, inc=1, device_id={"box": lax.rem(me + d, boxes)}, device_id_type=MESH
        )
        return 0

    lax.fori_loop(1, boxes, greet, 0)
    for peer in peers:
        pl.semaphore_signal(barrier, inc=1, device_id=peer, device_id_type=MESH)
    for copy in raw_in:
        copy.start()

    lane8 = iota((8, 128), 1)

    def window(d):
        b = lax.rem(me + d, boxes)
        y0 = anchors[1, b] + sy * (ty // RATIO - 1)
        z0 = anchors[2, b]
        to_even = lax.rem(128 - z0, 128)
        to_odd = lax.rem(192 - z0, 128)
        parts = []
        last = pltpu.roll(slab[y0 + 2 * both], to_odd, 1)
        extra = jnp.where(lane8 < 64, pltpu.roll(last, 4 * both, 1), last)
        for m in range(both):
            even = pltpu.roll(slab[y0 + 2 * m], to_even, 1)
            odd = pltpu.roll(slab[y0 + 2 * m + 1], to_odd, 1)
            parts.append(jnp.where(lane8 < 64, even, odd))
            extra = jnp.where(lane8 // 2 == m, pltpu.roll(odd, 2 * m, 1) if m > 0 else odd, extra)
            extra = jnp.where(lane8 // 2 == both + m, pltpu.roll(even, 64 + 2 * (both + m), 1), extra)
        return parts + [extra]

    def pack_window(d, _):
        for m, part in enumerate(window(d + 1)):
            packed[d + 1, m] = part
        return 0

    def send_window(d, _):
        pltpu.make_async_remote_copy(
            src_ref=packed.at[d],
            dst_ref=arrived.at[d],
            send_sem=pack_send,
            recv_sem=pack_recv,
            device_id={"box": lax.rem(me + d, boxes)},
            device_id_type=MESH,
        ).start()
        return 0

    odd_tile = (iota((ty, 128), 0) + iota((ty, 128), 1)) % 2 == 1
    odd_tall = (iota((ty + 16, 128), 0) + iota((ty + 16, 128), 1)) % 2 == 1
    odd8 = (iota((8, 128), 0) + iota((8, 128), 1)) % 2 == 1
    odd_line = (iota((pairs + 2, 128), 1) + y_edge) % 2 == 1

    halo_src = [[sxs, sys, sds], [dxs, dys, dds]]
    halo_dst = [[sxr, syr, sdr], [dxr, dyr, ddr]]

    def halo_copies(slot):
        return [
            pltpu.make_async_remote_copy(
                src_ref=halo_src[slot][n], dst_ref=halo_dst[slot][n],
                send_sem=halo_send.at[3 * slot + n], recv_sem=halo_recv.at[3 * slot + n],
                device_id=peers[n], device_id_type=MESH,
            )
            for n in range(3)
        ]

    def around(ref, ends, colour, kk, r0, rows, odd):
        lane = iota((rows, 128), 1)
        here = pl.ds(r0 + 8, rows)
        b = [ref[h, kk, here, :] for h in range(2)]
        below, above = along_z(b, ends, lane)
        result = []
        for h in range(2):
            before = ref[h, kk - 1, here, :]
            after = ref[h, kk + 1, here, :]
            side = jnp.where(odd, after, before) if colour == 0 else jnp.where(odd, before, after)
            result.append([
                b[h], side, ref[h, kk, pl.ds(r0 + 7, rows), :], ref[h, kk, pl.ds(r0 + 9, rows), :],
                below[h], above[h],
            ])
        return result

    def along_z(b, ends, lane):
        up = [pltpu.roll(v, 1, 1) for v in b]
        down = [pltpu.roll(v, 127, 1) for v in b]
        below = [jnp.where(lane == 0, ends, up[0]), jnp.where(lane == 0, up[0], up[1])]
        above = [jnp.where(lane == 127, down[1], down[0]), jnp.where(lane == 127, ends, down[1])]
        return below, above

    def around_line(mid, near, far, ends, odd_first):
        b = [mid[h, line_pairs, :] for h in range(2)]
        below, above = along_z(b, ends, iota((pairs + 2, 128), 1))
        result = []
        for h in range(2):
            before = mid[h, pl.ds(0, pairs + 2), :]
            after = mid[h, pl.ds(2, pairs + 2), :]
            side = jnp.where(odd_line, after, before) if odd_first else jnp.where(odd_line, before, after)
            result.append([b[h], side, near[h, line_pairs, :], far[h, line_pairs, :], below[h], above[h]])
        return result

    R0, R1, R2, B0, B1, B2, B3 = range(7)
    updates = ((R1, B1, B0, B2, False), (R2, B2, B1, B3, True), (B1, R1, R0, R2, True))

    def rows_to(dst, ref, row, first):
        for h in range(2):
            for k in range(pairs):
                dst[h, k : k + 1, :] = ref[h, k + first, pl.ds(row, 1), :]

    def line_to(dst, ref, row):
        for h in range(2):
            for k in range(pairs + 4):
                dst[h, k : k + 1, :] = ref[h, k, pl.ds(row, 1), :]

    def rows_from(src, first, ref, row):
        for h in range(2):
            for k in range(pairs):
                ref[h, k + 2, pl.ds(row, 1), :] = src[h, k + first : k + first + 1, :]

    zero_tall = jnp.zeros((ty + 16, 128), F32)

    def clear(kk, _):
        for h in range(2):
            er[h, kk] = zero_tall
            eb[h, kk] = zero_tall
        return 0

    lax.fori_loop(0, pairs + 4, clear, 0)
    sds[...] = jnp.zeros((16, 128), F32)
    dds[...] = jnp.zeros((8, 128), F32)

    def split(ref, k, h):
        low = ref[2 * k, :, pl.ds(128 * h, 128)]
        high = ref[2 * k + 1, :, pl.ds(128 * h, 128)]
        return jnp.where(odd_tile, high, low), jnp.where(odd_tile, low, high)

    def split_eps(k, _):
        for h in range(2):
            er[h, k + 2, 8:top, :], eb[h, k + 2, 8:top, :] = split(raw_e, k, h)
        return 0

    def split_rest(k, _):
        for h in range(2):
            for src, dst in ((raw_k, scr), (raw_s, chg)):
                dst[0, h, k], dst[1, h, k] = split(src, k, h)
        return 0

    anchor_in.wait()
    for copy in slab_in:
        copy.wait()
    loop(boxes - 1, pack_window, 0, 4)
    edge_row = pl.multiple_of((ty - 8) * (1 - sy), 8)
    edge_here = pl.ds(edge_row, 8)

    def split_edge(k, _):
        for h in range(2):
            halves = []
            for ref in (raw_e, raw_k, raw_s):
                low = ref[2 * k, edge_here, pl.ds(128 * h, 128)]
                high = ref[2 * k + 1, edge_here, pl.ds(128 * h, 128)]
                halves.append((jnp.where(odd8, high, low), jnp.where(odd8, low, high)))
            er[h, k + 2, pl.ds(edge_row + 8, 8), :], eb[h, k + 2, pl.ds(edge_row + 8, 8), :] = halves[0]
            scr[0, h, k, edge_here, :], scr[1, h, k, edge_here, :] = halves[1]
            chg[0, h, k, edge_here, :], chg[1, h, k, edge_here, :] = halves[2]
        return 0

    for copy in raw_in:
        copy.wait()
    loop(pairs, split_edge, 0, 4)
    for k in (x_edge - 2, x_next - 2):
        split_eps(k, 0)
        split_rest(k, 0)

    inward = [y_edge, y_edge - outward, y_edge - 2 * outward]
    for h in range(2):
        sxs[0, h] = er[h, x_edge, 8:top, :]
        sxs[1, h] = eb[h, x_edge, 8:top, :]
        sxs[2, h] = eb[h, x_next, 8:top, :]
        for colour in range(2):
            sxs[3 + 2 * colour, h] = scr[colour, h, x_edge - 2]
            sxs[4 + 2 * colour, h] = chg[colour, h, x_edge - 2]
        for n, (ref, row) in enumerate(((er, 0), (eb, 0), (eb, 1))):
            sds[2 * n + h : 2 * n + h + 1, :] = ref[h, x_edge, pl.ds(inward[row], 1), :]
        for n, ref in enumerate((scr, chg)):
            sds[6 + 2 * n + h : 7 + 2 * n + h, :] = ref[0, h, x_edge - 2, pl.ds(y_edge - 8, 1), :]
    for n, (ref, row) in enumerate(((er, 0), (er, 1), (eb, 0), (eb, 1), (eb, 2))):
        rows_to(sys.at[n], ref, inward[row], 2)
    for n, (ref, row) in enumerate(((scr.at[0], 0), (chg.at[0], 0), (scr.at[0], 1), (chg.at[0], 1), (scr.at[1], 0), (chg.at[1], 0))):
        rows_to(sys.at[5 + n], ref, inward[row] - 8, 0)
    pl.semaphore_wait(barrier, boxes - 1 + 3)
    for copy in halo_copies(0):
        copy.start()
    lax.fori_loop(1, boxes, send_window, 0)
    for m, part in enumerate(window(0)):
        arrived[0, m] = part

    loop(pairs, split_eps, 0, 2)
    loop(pairs, split_rest, 0, 2)
    def weigh(own, near):
        weights = [0.5 * (own + value) for value in near]
        return weights, sum(weights[1:], weights[0])

    def couple_rows(k, r0, rows, odd):
        here = pl.ds(r0, rows)
        for colour, mine, other in ((0, er, eb), (1, eb, er)):
            near = around(other, 0.0, colour, k + 2, r0, rows, odd)
            for h in range(2):
                weights, total = weigh(mine[h, k + 2, pl.ds(r0 + 8, rows), :], near[h])
                for n in range(6):
                    w[colour, n, h, k, here, :] = weights[n]
                diag[colour, h, k, here, :] = total

    def couple(k, _):
        couple_rows(k, 0, ty, odd_tile)
        return 0

    def couple_edge(k, _):
        couple_rows(k, edge_row, 8, odd8)
        return 0

    loop(pairs, couple, 0, 2)
    row = iota((128, 128), 0)
    col = iota((128, 128), 1)
    pz = []
    for h in range(3):
        if h < 2:
            q = col + 128 * h + 1
        else:
            q = jnp.where(col == 0, 0, 257)
        low = q // RATIO
        part = (q - low * RATIO).astype(F32) / RATIO
        pz.append(
            (jnp.where(row == low, 1.0 - part, 0.0) + jnp.where(row == low + 1, part, 0.0)).astype(jnp.bfloat16)
        )

    pltpu.make_async_copy(arrived.at[pl.ds(1, boxes - 1)], arrived.at[pl.ds(1, boxes - 1)], pack_recv).wait()
    row0 = anchors[0, me] + sx * (tx // RATIO - 1)
    first = row0 // 8
    phase = row0 - first * 8
    for t in range(deep // 8 - 1):
        holder = jnp.minimum(first + t, boxes - 1)
        slot = lax.rem(me - holder + boxes, boxes)
        extra = arrived[slot, both]
        for m in range(both):
            part = arrived[slot, m]
            odd_ends = pltpu.roll(extra, 128 - 2 * m, 1) if m > 0 else extra
            even_ends = pltpu.roll(extra, 64 - 2 * (both + m), 1)
            even = jnp.where(lane8 < 64, part, even_ends)
            odd = pltpu.roll(jnp.where(lane8 < 64, odd_ends, part), 64, 1)
            zin[pl.ds((2 * m) * deep + 8 * t + 8, 8), :] = even
            zin[pl.ds((2 * m + 1) * deep + 8 * t + 8, 8), :] = odd
        last = jnp.where(lane8 < 64, pltpu.roll(extra, 128 - 4 * both, 1), extra)
        zin[pl.ds(2 * both * deep + 8 * t + 8, 8), :] = pltpu.roll(last, 64, 1)
    for c in range(ncols):
        zin[pl.ds(c * deep, 8), :] = jnp.zeros((8, 128), F32)
    values = zin[...]
    split_parts = []
    for _ in range(3):
        part = values.astype(jnp.bfloat16)
        split_parts.append(part)
        values = values - part.astype(F32)
    for h in range(3):
        zfine[h] = sum(jnp.dot(part, pz[h], preferred_element_type=F32) for part in reversed(split_parts))

    for h in range(3):
        columns = [
            zfine[h, pl.ds(jnp.maximum(c + sy, 0) * deep + 7 + phase + sx, lines), :] for c in range(-1, ncols - 1)
        ]
        for q in range(-2, ty + 4):
            low, part = q // RATIO, (q % RATIO) / RATIO
            value = columns[low + 1]
            if part > 0:
                value = (1.0 - part) * value + part * columns[low + 2]
            ylines[h, pl.ds((q + 7) * lines, lines), :] = value
    for h in range(3):
        for r in range(nrows):
            xlines[h, r] = ylines[h, pl.ds(r, ty + 16, stride=lines), :]

    def guess(m, _):
        for h in range(3):
            here = xlines[h, m]
            after = xlines[h, m + 1]
            planes = (
                (2 * m, 0.75 * here + 0.25 * after, 0.5 * here + 0.5 * after),
                (2 * m + 1, 0.25 * here + 0.75 * after, after),
            )
            for kk, low, high in planes:
                red = jnp.where(odd_tall, high, low)
                black = jnp.where(odd_tall, low, high)
                if h < 2:
                    ur[h, kk] = red
                    ub[h, kk] = black
                else:
                    uend[0, kk] = red
                    uend[1, kk] = black
        return 0

    loop(pairs // 2 + 2, guess, 0, 2)

    def hyperbolic(value):
        power = value * LOG2E
        plus = jnp.exp2(power - 1.0)
        minus = jnp.exp2(-1.0 - power)
        return plus - minus, plus + minus

    def weighted(weights, near):
        total = weights(0) * near[0]
        for n in (4, 5, 1, 2, 3):
            total = total + weights(n) * near[n]
        return total

    def newton(centre, pull, main, salt):
        sinh, cosh = hyperbolic(centre)
        return centre - (main * centre - pull + salt * sinh) / (main + salt * cosh)

    def square(centre, pull, main, salt):
        g = main * centre - pull + salt * hyperbolic(centre)[0]
        return g * g

    def cells_of(colour, kk, r0, acc, update, residual):
        here = pl.ds(r0, 8)
        own, other = (ur, ub) if colour == 0 else (ub, ur)
        k = kk - 2
        near = around(other, uend[colour, kk, pl.ds(r0 + 8, 8), :], colour, kk, r0, 8, odd8)
        for h in range(2):
            pull = weighted(lambda n: w[colour, n, h, k, here, :], near[h]) + chg[colour, h, k, here, :]
            main = diag[colour, h, k, here, :]
            salt = scr[colour, h, k, here, :]
            value = own[h, kk, pl.ds(r0 + 8, 8), :]
            if update:
                value = newton(value, pull, main, salt)
                own[h, kk, pl.ds(r0 + 8, 8), :] = value
            if residual:
                acc = acc + square(value, pull, main, salt)
        return acc

    tiles = ty // 8
    rim = min(2, tiles)
    inner_pair = 2 + sx
    free_pair = 2 + 2 * sx
    rim_pair = x_edge - 1 + 2 * sx
    inner_row = pl.multiple_of(8 * sy, 8)
    free_row = pl.multiple_of(16 * sy, 8)
    rim_row = pl.multiple_of(8 * (tiles - rim) * (1 - sy), 8)
    near_row = pl.multiple_of(8 * sy + 8 * (tiles - rim) * (1 - sy), 8)

    def edge(colour, acc, residual):
        for r0 in range(0, ty, 8):
            acc = cells_of(colour, x_edge, r0, acc, True, residual)
        return loop(
            pairs - 1,
            lambda i, acc: cells_of(colour, inner_pair + i, edge_row, acc, True, residual),
            acc, pairs,
        )

    def interior(colour, acc, residual):
        def step(i, acc):
            for s in range(tiles - 1):
                acc = cells_of(colour, inner_pair + i, pl.multiple_of(inner_row + 8 * s, 8), acc, True, residual)
            return acc

        return loop(pairs - 1, step, acc, 5)

    def rim_of(colour, acc):
        for s in range(tiles - 1):
            acc = cells_of(colour, rim_pair, pl.multiple_of(inner_row + 8 * s, 8), acc, True, False)
        if tiles < 2:
            return acc
        return loop(
            pairs - 2, lambda i, acc: cells_of(colour, free_pair + i, near_row, acc, True, False), acc, pairs
        )

    def free(colour, acc, update, residual):
        def step(i, acc):
            for s in range(tiles - rim):
                acc = cells_of(colour, free_pair + i, pl.multiple_of(free_row + 8 * s, 8), acc, update, residual)
            return acc

        return loop(pairs - 2, step, acc, 6)

    def send_red():
        for h in range(2):
            dxs[h] = ur[h, x_edge, 8:top, :]
            dds[h : h + 1, :] = ur[h, x_edge, pl.ds(y_edge, 1), :]
        for n in range(2):
            rows_to(dys.at[n], ur, inward[n], 2)
        for copy in halo_copies(1):
            copy.start()

    def take_red():
        for copy in halo_copies(1):
            copy.wait_recv()
        for h in range(2):
            ur[h, x_halo, 8:top, :] = dxr[h]
            for n in range(2):
                lu[R1 + n, h, own_pairs, :] = dyr[n, h]
            lu[R0, h, own_pairs, :] = dys[0, h]
            lu[R1, h, pl.ds(x_halo, 1), :] = ddr[h : h + 1, :]

    def spread_red():
        for h in range(2):
            ur[h, x_halo, pl.ds(outer_rows[1], 1), :] = lu[R1, h, pl.ds(x_halo, 1), :]
        rows_from(lu.at[R1], 2, ur, outer_rows[1])

    def line_step(i):
        own, mid, near, far, odd_first = updates[i]
        near = around_line(lu.at[mid], lu.at[near], lu.at[far], lend[i, line_pairs, :], odd_first)
        for h in range(2):
            pull = weighted(lambda n: wl[i, n, h], near[h]) + sl[i, h]
            edge_value = lu[own, h, pl.ds(x_far, 1), :]
            lu[own, h, line_pairs, :] = newton(lu[own, h, line_pairs, :], pull, dl[i, h], kl[i, h])
            lu[own, h, pl.ds(x_far, 1), :] = edge_value

    def pair_step(colour):
        mine, other = (ur, ub) if colour == 0 else (ub, ur)
        near = around(other, uend[colour, x_halo, 8:top, :], colour, x_halo, 0, ty, odd_tile)
        for h in range(2):
            pull = weighted(lambda n: wx[colour, n, h], near[h]) + sxr[4 + 2 * colour, h]
            mine[h, x_halo, 8:top, :] = newton(mine[h, x_halo, 8:top, :], pull, dx[colour, h], sxr[3 + 2 * colour, h])

    def black_beside():
        pair_step(1)
        line_step(2)
        rows_from(lu.at[B1], 2, ub, outer_rows[1])

    total = jnp.zeros((8, 128), F32)
    interior(0, total, False)

    for copy in halo_copies(0):
        copy.wait_recv()
    outer_rows = [y_edge + n * outward for n in range(4)]
    for h in range(2):
        er[h, x_halo, 8:top, :] = sxr[0, h]
        eb[h, x_halo, 8:top, :] = sxr[1, h]
        eb[h, x_outer, 8:top, :] = sxr[2, h]
        for n, (ref, row) in enumerate(((er, 1), (eb, 1), (eb, 2))):
            ref[h, x_halo, pl.ds(outer_rows[row], 1), :] = sdr[2 * n + h : 2 * n + h + 1, :]
    for n, (ref, row) in enumerate(((er, 1), (er, 2), (eb, 1), (eb, 2), (eb, 3))):
        rows_from(syr.at[n], 0, ref, outer_rows[row])
    for n in range(3):
        for h in range(2):
            kl[n, h, pl.ds(1, pairs), :] = syr[5 + 2 * n, h]
            sl[n, h, pl.ds(1, pairs), :] = syr[6 + 2 * n, h]
    for h in range(2):
        kl[0, h, pl.ds(x_halo - 1, 1), :] = sdr[6 + h : 7 + h, :]
        sl[0, h, pl.ds(x_halo - 1, 1), :] = sdr[8 + h : 9 + h, :]
    for n in range(7):
        line_to(le.at[n], er if n < 3 else eb, outer_rows[n if n < 3 else n - 3])
    loop(pairs, couple_edge, 0, 5)
    couple(x_edge - 2, 0)
    for colour, mine, other in ((0, er, eb), (1, eb, er)):
        near = around(other, 0.0, colour, x_halo, 0, ty, odd_tile)
        for h in range(2):
            weights, dx[colour, h] = weigh(mine[h, x_halo, 8:top, :], near[h])
            for n in range(6):
                wx[colour, n, h] = weights[n]
    for i, (own, mid, near, far, odd_first) in enumerate(updates):
        near = around_line(le.at[mid], le.at[near], le.at[far], 0.0, odd_first)
        for h in range(2):
            weights, dl[i, h] = weigh(le[own, h, line_pairs, :], near[h])
            for n in range(6):
                wl[i, n, h] = weights[n]

    for n in range(7):
        line_to(lu.at[n], ur if n < 3 else ub, outer_rows[n if n < 3 else n - 3])
    for i, (colour, row) in enumerate(((0, 1), (0, 2), (1, 1))):
        for k in range(pairs + 4):
            lend[i, k : k + 1, :] = uend[colour, k, pl.ds(outer_rows[row], 1), :]
    edge(0, total, False)
    pair_step(0)
    line_step(0)
    line_step(1)
    spread_red()
    line_to(lu.at[R0], ur, y_edge)
    black_beside()
    edge(1, total, False)
    rim_of(1, total)
    edge(0, total, False)
    send_red()
    free(1, total, True, False)
    interior(0, total, False)
    total = interior(1, total, True)
    total = free(0, total, False, True)
    take_red()
    spread_red()
    black_beside()
    total = edge(1, total, True)

    def residual_rim(i, acc):
        for s in range(rim):
            acc = cells_of(0, free_pair + i, pl.multiple_of(rim_row + 8 * s, 8), acc, False, True)
        return acc

    for i in range(2):
        for r0 in range(0, ty, 8):
            total = cells_of(0, (pairs - 2) * (1 - sx) + 2 + i, r0, total, False, True)
    sums[group] = loop(pairs - 2, residual_rim, total, 6)
    sum_copies = [
        pltpu.make_async_remote_copy(
            src_ref=sums.at[group], dst_ref=sums.at[group],
            send_sem=ss_sem.at[n], recv_sem=sr_sem.at[n],
            device_id=peer, device_id_type=MESH,
        )
        for n, peer in enumerate(peers)
    ]
    for copy in sum_copies:
        copy.start()

    def join(k, _):
        for h in range(2):
            red = ur[h, k + 2, 8:top, :]
            black = ub[h, k + 2, 8:top, :]
            pot[0, 2 * k, :, pl.ds(128 * h, 128)] = jnp.where(odd_tile, black, red)
            pot[0, 2 * k + 1, :, pl.ds(128 * h, 128)] = jnp.where(odd_tile, red, black)
        return 0

    loop(pairs, join, 0, 2)

    pltpu.make_async_copy(packed.at[pl.ds(1, boxes - 1)], packed.at[pl.ds(1, boxes - 1)], pack_send).wait()
    for slot in range(2):
        for copy in halo_copies(slot):
            copy.wait_send()
    for copy in sum_copies:
        copy.wait()
    squares = jnp.sum(sums[0] + sums[1] + sums[2] + sums[3], keepdims=True)
    norm_out[...] = jnp.sqrt(squares / cells + 1e-06)


def body(coarse, anchors, dielectric, screening, source):
    boxes = lax.axis_size("box")
    _, tx, ty, tz = dielectric.shape
    pairs = tx // 2
    nrows = pairs // 2 + 3
    ncols = ty // RATIO + 3
    deep = (nrows + 14) // 8 * 8 + 8
    lines = (nrows + 7) // 8 * 8
    slabs, gy, gz = coarse.shape
    cells = tx * ty * tz * lax.axis_size("sx") * lax.axis_size("sy")
    any_spec = pl.BlockSpec(memory_space=pl.ANY)
    vmem_spec = pl.BlockSpec(memory_space=pltpu.VMEM)
    dma = pltpu.SemaphoreType.DMA

    def vmem(*shape):
        return pltpu.VMEM(shape, F32)

    def padded():
        return vmem(2, pairs + 4, ty + 16, 128)

    potential, norm = pl.pallas_call(
        functools.partial(kernel, boxes, tx, ty, cells),
        out_shape=(
            jax.ShapeDtypeStruct((1, tx, ty, tz), F32),
            jax.ShapeDtypeStruct((1, 1), F32),
        ),
        in_specs=[any_spec] * 5,
        out_specs=(vmem_spec, vmem_spec),
        scratch_shapes=[
            pltpu.SMEM((3, boxes), jnp.int32),
            vmem(gy, slabs, gz),
            vmem(boxes, ncols // 2 + 1, 8, 128),
            vmem(boxes, ncols // 2 + 1, 8, 128),
            vmem(ncols * deep, 128),
            vmem(3, ncols * deep, 128),
            vmem(3, (ty + 16) * lines, 128),
            vmem(3, nrows, ty + 16, 128),
            vmem(tx, ty, tz),
            vmem(tx, ty, tz),
            vmem(tx, ty, tz),
            padded(),
            padded(),
            vmem(2, 2, pairs, ty, 128),
            vmem(2, 2, pairs, ty, 128),
            vmem(2, 6, 2, pairs, ty, 128),
            vmem(2, 2, pairs, ty, 128),
            padded(),
            padded(),
            padded(),
            vmem(2, 6, 2, ty, 128),
            vmem(2, 2, ty, 128),
            vmem(3, 6, 2, pairs + 2, 128),
            vmem(3, 2, pairs + 2, 128),
            vmem(3, 2, pairs + 2, 128),
            vmem(3, 2, pairs + 2, 128),
            vmem(7, 2, pairs + 4, 128),
            vmem(7, 2, pairs + 4, 128),
            vmem(3, pairs + 4, 128),
            vmem(7, 2, ty, 128),
            vmem(7, 2, ty, 128),
            vmem(11, 2, pairs, 128),
            vmem(11, 2, pairs, 128),
            vmem(16, 128),
            vmem(16, 128),
            vmem(2, ty, 128),
            vmem(2, ty, 128),
            vmem(2, 2, pairs, 128),
            vmem(2, 2, pairs, 128),
            vmem(8, 128),
            vmem(8, 128),
            vmem(4, 8, 128),
            dma, dma((slabs,)), dma((3,)), dma, dma, dma((6,)), dma((6,)), dma((3,)), dma((3,)),
        ],
        compiler_params=pltpu.CompilerParams(
            collective_id=0, has_side_effects=True, vmem_limit_bytes=52 * 1024 * 1024
        ),
        cost_estimate=pl.CostEstimate(
            flops=200 * tx * ty * tz, bytes_accessed=16 * tx * ty * tz, transcendentals=12 * tx * ty * tz
        ),
    )(*(
        pltpu.with_memory_space_constraint(operand, pltpu.HBM)
        for operand in (anchors.T, coarse, dielectric, screening, source)
    ))
    return potential, norm.reshape(1)


def solution(mesh):
    tile = P("box", "sx", "sy", None)
    return jax.shard_map(
        body,
        mesh=mesh,
        in_specs=(P("box", None, None), P(), tile, tile, tile),
        out_specs=(tile, P("box")),
        check_vma=False,
    )
```

time: 40 us -> 37.2 us (0.930)
  Pallas kernels: 36.3 us -> 33.6 us
    pallas_call x1, Pallas kernels: 36.3 us -> 33.6 us  [body(): pl.pallas_call(functools.partial(kernel, boxes, tx, ty, cells), out_shape...]
where the time goes in v4:
time: 37.2 us; the launch traced here: 37 us
  Pallas kernels  33.6 us (90%)
  between operations  2.33 us (6%)
  local copies, waits for them, and re-layouts  1.06 us (3%)
    pallas_call x1, Pallas kernels, body(): pl.pallas_call(functools.partial(kernel, boxes, tx, ty, cells), out_shape...  33.6 us
    unnamed x1, local copies, waits for them, and re-layouts  1.06 us

profile of v4, /device:TPU:96, one launch (start us, length us, event | category | flops | bytes accessed | tf_op | source)
XLA Modules:
  0.0 37.0 jit_solution(8351969940126784241)
XLA Ops:
  0.6 33.6 %shard_map.68 = (f32[1,40,32,256]{3,2,1,0:T(8,128)S(1)}, f32[1,1]{1,0:T(1,128)}) custom-call(s32[3,32]{1,0:T(4,128)} %bitcast.2, f32[8,96,128]{2,1,0:T(8,128)} %coarse.1, f32[1,40,32,256]{3,2,1,0:T(8,128)} %diel.1, f32[1,40,32,256]{3,2,1,0:T(8,128)} %screen.1, f32[1,40,32,256]{3,2,1,0:T(8,128)} %source.1), custom_call_target="tpu_custom_call" | custom-call | flops 65536000 | bytes 5242880 | tf_op jit(solution)/shard_map/pallas_call | solution.py:629
  34.3 1.1 %copy.9 = f32[1,40,32,256]{3,2,1,0:T(8,128)} copy(f32[1,40,32,256]{3,2,1,0:T(8,128)S(1)} %get-tuple-element.8) | data formatting | bytes 2621440

commit v5 on v4

--- a/solution.py
+++ b/solution.py
@@ -207,6 +207,9 @@
 
     lax.fori_loop(0, pairs + 4, clear, 0)
     sds[...] = jnp.zeros((16, 128), F32)
+    for n in range(7):
+        for h in range(2):
+            le[n, h] = jnp.zeros((pairs + 4, 128), F32)
     dds[...] = jnp.zeros((8, 128), F32)
 
     def split(ref, k, h):
@@ -312,6 +315,8 @@
         pz.append(
             (jnp.where(row == low, 1.0 - part, 0.0) + jnp.where(row == low + 1, part, 0.0)).astype(jnp.bfloat16)
         )
+
+    pz_all = jnp.concatenate([jnp.concatenate(pz, axis=1)] * 3, axis=0)
 
     pltpu.make_async_copy(arrived.at[pl.ds(1, boxes - 1)], arrived.at[pl.ds(1, boxes - 1)], pack_recv).wait()
     row0 = anchors[0, me] + sx * (tx // RATIO - 1)
@@ -339,8 +344,9 @@
         part = values.astype(jnp.bfloat16)
         split_parts.append(part)
         values = values - part.astype(F32)
+    product = jnp.dot(jnp.concatenate(split_parts, axis=1), pz_all, preferred_element_type=F32)
     for h in range(3):
-        zfine[h] = sum(jnp.dot(part, pz[h], preferred_element_type=F32) for part in reversed(split_parts))
+        zfine[h] = product[:, 128 * h : 128 * h + 128]
 
     for h in range(3):
         columns = [
@@ -515,8 +521,8 @@
         eb[h, x_outer, 8:top, :] = sxr[2, h]
         for n, (ref, row) in enumerate(((er, 1), (eb, 1), (eb, 2))):
             ref[h, x_halo, pl.ds(outer_rows[row], 1), :] = sdr[2 * n + h : 2 * n + h + 1, :]
-    for n, (ref, row) in enumerate(((er, 1), (er, 2), (eb, 1), (eb, 2), (eb, 3))):
-        rows_from(syr.at[n], 0, ref, outer_rows[row])
+    rows_from(syr.at[0], 0, er, outer_rows[1])
+    rows_from(syr.at[2], 0, eb, outer_rows[1])
     for n in range(3):
         for h in range(2):
             kl[n, h, pl.ds(1, pairs), :] = syr[5 + 2 * n, h]
@@ -524,8 +530,13 @@
     for h in range(2):
         kl[0, h, pl.ds(x_halo - 1, 1), :] = sdr[6 + h : 7 + h, :]
         sl[0, h, pl.ds(x_halo - 1, 1), :] = sdr[8 + h : 9 + h, :]
-    for n in range(7):
-        line_to(le.at[n], er if n < 3 else eb, outer_rows[n if n < 3 else n - 3])
+    for n, ref in ((R0, sys.at[0]), (R1, syr.at[0]), (R2, syr.at[1]), (B0, sys.at[2]), (B1, syr.at[2]), (B2, syr.at[3]), (B3, syr.at[4])):
+        for h in range(2):
+            le[n, h, own_pairs, :] = ref[h]
+    for h in range(2):
+        for n, line in enumerate((R1, B1, B2)):
+            le[line, h, pl.ds(x_halo, 1), :] = sdr[2 * n + h : 2 * n + h + 1, :]
+        le[B0, h, pl.ds(x_halo, 1), :] = sxr[1, h, pl.ds(y_edge - 8, 1), :]
     loop(pairs, couple_edge, 0, 5)
     couple(x_edge - 2, 0)
     for colour, mine, other in ((0, er, eb), (1, eb, er)):
@@ -541,7 +552,7 @@
             for n in range(6):
                 wl[i, n, h] = weights[n]
 
-    for n in range(7):
+    for n in range(1, 7):
         line_to(lu.at[n], ur if n < 3 else ub, outer_rows[n if n < 3 else n - 3])
     for i, (colour, row) in enumerate(((0, 1), (0, 2), (1, 1))):
         for k in range(pairs + 4):

time: 37.2 us -> 37 us (level)
  no operation moved by 1% of the time
where the time goes in v5:
time: 37 us; the launch traced here: 36.9 us
  Pallas kernels  33.5 us (91%)
  between operations  2.33 us (6%)
  local copies, waits for them, and re-layouts  1.06 us (3%)
    pallas_call x1, Pallas kernels, body(): pl.pallas_call(functools.partial(kernel, boxes, tx, ty, cells), out_shape...  33.5 us
    unnamed x1, local copies, waits for them, and re-layouts  1.06 us

profile of v5, /device:TPU:96, one launch (start us, length us, event | category | flops | bytes accessed | tf_op | source)
XLA Modules:
  0.0 36.9 jit_solution(8788765066581090555)
XLA Ops:
  0.6 33.5 %shard_map.68 = (f32[1,40,32,256]{3,2,1,0:T(8,128)S(1)}, f32[1,1]{1,0:T(1,128)}) custom-call(s32[3,32]{1,0:T(4,128)} %bitcast.2, f32[8,96,128]{2,1,0:T(8,128)} %coarse.1, f32[1,40,32,256]{3,2,1,0:T(8,128)} %diel.1, f32[1,40,32,256]{3,2,1,0:T(8,128)} %screen.1, f32[1,40,32,256]{3,2,1,0:T(8,128)} %source.1), custom_call_target="tpu_custom_call" | custom-call | flops 65536000 | bytes 5242880 | tf_op jit(solution)/shard_map/pallas_call | solution.py:640
  34.1 1.1 %copy.9 = f32[1,40,32,256]{3,2,1,0:T(8,128)} copy(f32[1,40,32,256]{3,2,1,0:T(8,128)S(1)} %get-tuple-element.8) | data formatting | bytes 2621440

commit v6 on v5

--- a/solution.py
+++ b/solution.py
@@ -209,7 +209,7 @@
     sds[...] = jnp.zeros((16, 128), F32)
     for n in range(7):
         for h in range(2):
-            le[n, h] = jnp.zeros((pairs + 4, 128), F32)
+            le[n, h] = jnp.zeros((pairs + 12, 128), F32)
     dds[...] = jnp.zeros((8, 128), F32)
 
     def split(ref, k, h):
@@ -492,9 +492,9 @@
         own, mid, near, far, odd_first = updates[i]
         near = around_line(lu.at[mid], lu.at[near], lu.at[far], lend[i, line_pairs, :], odd_first)
         for h in range(2):
-            pull = weighted(lambda n: wl[i, n, h], near[h]) + sl[i, h]
+            pull = weighted(lambda n: wl[i, n, h], near[h]) + sl[i, h, 0 : pairs + 2, :]
             edge_value = lu[own, h, pl.ds(x_far, 1), :]
-            lu[own, h, line_pairs, :] = newton(lu[own, h, line_pairs, :], pull, dl[i, h], kl[i, h])
+            lu[own, h, line_pairs, :] = newton(lu[own, h, line_pairs, :], pull, dl[i, h], kl[i, h, 0 : pairs + 2, :])
             lu[own, h, pl.ds(x_far, 1), :] = edge_value
 
     def pair_step(colour):
@@ -635,7 +635,7 @@
         return pltpu.VMEM(shape, F32)
 
     def padded():
-        return vmem(2, pairs + 4, ty + 16, 128)
+        return vmem(2, pairs + 5, ty + 16, 128)
 
     potential, norm = pl.pallas_call(
         functools.partial(kernel, boxes, tx, ty, cells),
@@ -659,8 +659,8 @@
             vmem(tx, ty, tz),
             padded(),
             padded(),
-            vmem(2, 2, pairs, ty, 128),
-            vmem(2, 2, pairs, ty, 128),
+            vmem(2, 2, pairs + 1, ty, 128),
+            vmem(2, 2, pairs + 1, ty, 128),
             vmem(2, 6, 2, pairs, ty, 128),
             vmem(2, 2, pairs, ty, 128),
             padded(),
@@ -670,11 +670,11 @@
             vmem(2, 2, ty, 128),
             vmem(3, 6, 2, pairs + 2, 128),
             vmem(3, 2, pairs + 2, 128),
-            vmem(3, 2, pairs + 2, 128),
-            vmem(3, 2, pairs + 2, 128),
-            vmem(7, 2, pairs + 4, 128),
-            vmem(7, 2, pairs + 4, 128),
-            vmem(3, pairs + 4, 128),
+            vmem(3, 2, pairs + 12, 128),
+            vmem(3, 2, pairs + 12, 128),
+            vmem(7, 2, pairs + 12, 128),
+            vmem(7, 2, pairs + 12, 128),
+            vmem(3, pairs + 12, 128),
             vmem(7, 2, ty, 128),
             vmem(7, 2, ty, 128),
             vmem(11, 2, pairs, 128),

time: 37 us -> 37 us (level)
  no operation moved by 1% of the time
where the time goes in v6:
time: 37 us; the launch traced here: 36.9 us
  Pallas kernels  33.5 us (91%)
  between operations  2.33 us (6%)
  local copies, waits for them, and re-layouts  1.06 us (3%)
    pallas_call x1, Pallas kernels, body(): pl.pallas_call(functools.partial(kernel, boxes, tx, ty, cells), out_shape...  33.5 us
    unnamed x1, local copies, waits for them, and re-layouts  1.06 us

profile of v6, /device:TPU:96, one launch (start us, length us, event | category | flops | bytes accessed | tf_op | source)
XLA Modules:
  0.0 36.9 jit_solution(17119883862701561225)
XLA Ops:
  0.6 33.5 %shard_map.68 = (f32[1,40,32,256]{3,2,1,0:T(8,128)S(1)}, f32[1,1]{1,0:T(1,128)}) custom-call(s32[3,32]{1,0:T(4,128)} %bitcast.2, f32[8,96,128]{2,1,0:T(8,128)} %coarse.1, f32[1,40,32,256]{3,2,1,0:T(8,128)} %diel.1, f32[1,40,32,256]{3,2,1,0:T(8,128)} %screen.1, f32[1,40,32,256]{3,2,1,0:T(8,128)} %source.1), custom_call_target="tpu_custom_call" | custom-call | flops 65536000 | bytes 5242880 | tf_op jit(solution)/shard_map/pallas_call | solution.py:640
  34.1 1.1 %copy.9 = f32[1,40,32,256]{3,2,1,0:T(8,128)} copy(f32[1,40,32,256]{3,2,1,0:T(8,128)S(1)} %get-tuple-element.8) | data formatting | bytes 2621440
